TPU v7x, 128 devices: a whole 4x4x4 slice. The times are simulated.
128 devices in a mesh: seq: 8 (over z_hi, x), exp: 16 (over z_lo, y, core).
Axes of the slice: x: 4, y: 4, z: 4 (z_hi: 2, z_lo: 2; z = z_hi * 2 + z_lo), core: 2. Of those that a mesh axis runs over, the one named last changes fastest.
Arguments:
- tokens: bfloat16 [16, 2048, 768], P('exp', 'seq'), may hold values from -6 to 6
- cotangent: bfloat16 [16, 2048, 768], P('exp', 'seq'), may hold values from -6 to 6
- gain_first: float32 [768], replicated, may hold values from 0.1 to 1.9
- w_qkv: bfloat16 [768, 2304], replicated, may hold values from -0.21875 to 0.21875
- w_o: bfloat16 [768, 768], replicated, may hold values from -1.75 to 1.75
- gain_second: float32 [768], replicated, may hold values from 0.1 to 1.9
- w_gate: bfloat16 [768, 32], replicated, may hold values from -0.15625 to 0.15625
- w_in: bfloat16 [32, 768, 3072], P('exp', None, 'seq'), may hold values from -0.21875 to 0.21875
- w_out: bfloat16 [32, 3072, 768], P('exp', 'seq'), may hold values from -0.109375 to 0.109375
- routes: int32 [16, 2048, 2], P('exp', 'seq'), may hold values from 0 to 31, all different within a row; in each aligned block of 256 rows (0 to 255, 256 to 511, ..., all dimensions but the last counted through in order) at most 32 rows name the same one
- frozen: int32 [32], replicated, may hold values from 0 to 1, as said below
Outputs:
- out: bfloat16 [16, 2048, 768], P('exp', 'seq')
- tokens_grad: float32 [16, 2048, 768], P('exp', 'seq')
- gain_first_grad: float32 [768], replicated
- qkv_grad: float32 [768, 2304], replicated
- o_grad: float32 [768, 768], replicated
- gain_second_grad: float32 [768], replicated
- gate_grad: float32 [768, 32], replicated
- w_in_grad: float32 [32, 768, 3072], P('exp', None, 'seq')
- w_out_grad: float32 [32, 3072, 768], P('exp', 'seq')
Inputs may be any that keep to these rules, and one draw needn't show every extreme that they name: `routes`: A token's two experts differ. In each aligned block of 256 positions of a sequence no expert is named more than 32 times, and in some block some expert exactly 32 times; every expert is named somewhere. Half of the 32 experts are frozen.
All inputs are finite; a program needn't handle non-finite values.
Results may differ from a plain program's by a relative error of at most 0.015.
Values may be sent and summed in bfloat16 or wider, within the bound.
A program may use at most 256 MiB of HBM per device.

v0:
```python
import jax
import jax.numpy as jnp
from jax import lax
from jax.sharding import PartitionSpec as P

HEADS = 12
HEAD_DIM = 64
EXPERTS = 32
CAP = 32


exact_mode = lax.Precision.HIGHEST
epsilon = 1e-05


def norm_forward(values, gain_vec):
    centred = values - jnp.mean(values, axis=-1, keepdims=True)
    inv_scale = lax.rsqrt(jnp.mean(centred * centred, axis=-1, keepdims=True) + epsilon)
    normed = centred * inv_scale
    return (normed * gain_vec, normed, inv_scale)


def norm_backward(gradient, gain_vec, normed, inv_scale):
    scaled = gradient * gain_vec
    softmax_dot_correction = jnp.mean(scaled, axis=-1, keepdims=True)
    cross_term = jnp.mean(scaled * normed, axis=-1, keepdims=True)
    return (
        inv_scale * (scaled - softmax_dot_correction - normed * cross_term),
        jnp.sum(gradient * normed, axis=(0, 1)),
    )


def split_heads(values):
    seq_count, row_count, model_width = values.shape
    return values.reshape(seq_count, row_count, HEADS, model_width // HEADS).transpose(2, 0, 1, 3)


def merge_heads(values):
    head_count, seq_count, row_count, head_width = values.shape
    return values.transpose(1, 2, 0, 3).reshape(seq_count, row_count, head_count * head_width)


def head_forward(operands, allowed):
    asking_token_vectors, key_matrix_rows, value_matrix_rows = operands
    scores = jnp.einsum(
        "yrx,ylx->yrl", asking_token_vectors, key_matrix_rows, preferred_element_type=jnp.float32
    ) * HEAD_DIM ** (-0.5)
    scores = jnp.where(allowed[None], scores, -1e30)
    row_max = jnp.max(scores, axis=-1, keepdims=True)
    exponent = jnp.exp(scores - row_max)
    row_total = jnp.sum(exponent, axis=-1, keepdims=True)
    weight_params = (exponent / row_total).astype(jnp.bfloat16)
    block_output = jnp.einsum(
        "pnx,pxi->pni", weight_params, value_matrix_rows, preferred_element_type=jnp.float32
    )
    return (block_output, row_max[..., 0] + jnp.log(row_total[..., 0]))


def head_backward(operands, allowed):
    asking_token_vectors, key_matrix_rows, value_matrix_rows, result_cotangent, log_total = operands
    scores = jnp.einsum(
        "yrx,ylx->yrl", asking_token_vectors, key_matrix_rows, preferred_element_type=jnp.float32
    ) * HEAD_DIM ** (-0.5)
    scores = jnp.where(allowed[None], scores, -1e30)
    weight_params = jnp.exp(scores - log_total[..., None])
    truncated_entries = weight_params.astype(jnp.bfloat16)
    value_grad = jnp.einsum(
        "azn,azj->anj", truncated_entries, result_cotangent, preferred_element_type=jnp.float32
    )
    weight_grad = jnp.einsum(
        "yrx,ylx->yrl", result_cotangent, value_matrix_rows, preferred_element_type=jnp.float32
    )
    softmax_dot_correction = jnp.sum(weight_grad * weight_params, axis=-1, keepdims=True)
    logit_cotangent = (weight_params * (weight_grad - softmax_dot_correction)).astype(jnp.bfloat16)
    query_grad = jnp.einsum(
        "pnx,pxi->pni", logit_cotangent, key_matrix_rows, preferred_element_type=jnp.float32
    ) * HEAD_DIM ** (-0.5)
    key_grad = jnp.einsum(
        "azn,azj->anj", logit_cotangent, asking_token_vectors, preferred_element_type=jnp.float32
    ) * HEAD_DIM ** (-0.5)
    return (query_grad, key_grad, value_grad)


def slot_table(routes):
    seq_count, row_count, _ = routes.shape
    flat_ids = routes.reshape(seq_count, row_count * 2)
    matches = (flat_ids[..., None] == jnp.arange(EXPERTS, dtype=jnp.int32)).astype(jnp.int32)
    earlier = jnp.cumsum(matches, axis=1) - matches
    slot_number = jnp.sum(earlier * matches, axis=-1)
    return (flat_ids * CAP + slot_number).reshape(seq_count, row_count, 2)


def on_device(
    tokens, cotangent, gain_first, w_qkv, w_o, gain_second, w_gate, w_in, w_out, routes, frozen
):
    seq_count, row_count, model_width = tokens.shape
    full_length = row_count * lax.axis_size("seq")
    offset = lax.axis_index("seq") * row_count
    allowed = (offset + jnp.arange(row_count, dtype=jnp.int32))[:, None] >= jnp.arange(
        full_length, dtype=jnp.int32
    )[None, :]
    inputs = tokens.astype(jnp.float32)
    normed_one, unit_one, scale_one = norm_forward(inputs, gain_first)
    acts_one = normed_one.astype(jnp.bfloat16)
    joined = jnp.einsum("bld,de->ble", acts_one, w_qkv, preferred_element_type=jnp.float32).astype(
        jnp.bfloat16
    )
    asking_token_vectors = joined[..., :model_width]
    key_matrix_rows = joined[..., model_width : 2 * model_width]
    value_matrix_rows = joined[..., 2 * model_width :]
    gathered = (
        lax.all_gather(key_matrix_rows, "seq", axis=1, tiled=True),
        lax.all_gather(value_matrix_rows, "seq", axis=1, tiled=True),
    )
    query_heads = split_heads(asking_token_vectors)
    head_out, log_total = lax.map(
        lambda operands: head_forward(operands, allowed),
        (query_heads, split_heads(gathered[0]), split_heads(gathered[1])),
    )
    attended = merge_heads(head_out).astype(jnp.bfloat16)
    branch = jnp.einsum("bld,de->ble", attended, w_o, preferred_element_type=jnp.float32)
    mid = inputs + branch
    normed_two, unit_two, scale_two = norm_forward(mid, gain_second)
    acts_two = normed_two.astype(jnp.bfloat16)
    logits = jnp.einsum("bld,de->ble", acts_two, w_gate, preferred_element_type=jnp.float32)
    expert_range = jnp.arange(EXPERTS, dtype=jnp.int32)
    choose_first = (routes[..., 0:1] == expert_range).astype(jnp.float32)
    choose_second = (routes[..., 1:2] == expert_range).astype(jnp.float32)
    picked = jnp.stack(
        [jnp.sum(logits * choose_first, axis=-1), jnp.sum(logits * choose_second, axis=-1)], axis=-1
    )
    gates = jax.nn.softmax(picked, axis=-1)
    slot_index = slot_table(routes)
    columns = jnp.arange(EXPERTS * CAP, dtype=jnp.int32)
    first_sel = (
        (slot_index[..., 0:1] == columns)
        .astype(jnp.float32)
        .reshape(seq_count, row_count, EXPERTS, CAP)
    )
    runner_up_mask = (
        (slot_index[..., 1:2] == columns)
        .astype(jnp.float32)
        .reshape(seq_count, row_count, EXPERTS, CAP)
    )
    either_sel = first_sel + runner_up_mask
    send_rows = jnp.einsum(
        "blec,bld->ebcd",
        either_sel.astype(jnp.bfloat16),
        acts_two,
        preferred_element_type=jnp.float32,
    )
    send_rows = send_rows.astype(jnp.bfloat16).reshape(EXPERTS, seq_count * CAP, model_width)
    owned = lax.all_to_all(send_rows, "exp", split_axis=0, concat_axis=1, tiled=True)
    expert_in = lax.all_gather(owned, "seq", axis=1, tiled=True)
    first_weight, second_weight = (w_in, w_out)
    pre_act = jnp.einsum(
        "erd,edf->erf", expert_in, first_weight, preferred_element_type=jnp.float32
    )
    hidden = jax.nn.gelu(pre_act, approximate=False).astype(jnp.bfloat16)
    partial_out = jnp.einsum(
        "erf,efd->erd", hidden, second_weight, preferred_element_type=jnp.float32
    )
    expert_out = lax.psum_scatter(
        partial_out.astype(jnp.bfloat16), "seq", scatter_dimension=1, tiled=True
    )
    returned = lax.all_to_all(expert_out, "exp", split_axis=1, concat_axis=0, tiled=True)
    returned = returned.reshape(EXPERTS, seq_count, CAP, model_width).astype(jnp.float32)
    from_first = jnp.einsum("blec,ebcd->bld", first_sel, returned, precision=exact_mode)
    from_second = jnp.einsum("blec,ebcd->bld", runner_up_mask, returned, precision=exact_mode)
    mixed_out = gates[..., 0:1] * from_first + gates[..., 1:2] * from_second
    result = mid + mixed_out
    gradient = cotangent.astype(jnp.float32)
    leading_expert_share = jnp.sum(gradient * from_first, axis=-1)
    gate_second = jnp.sum(gradient * from_second, axis=-1)
    logit_delta = (leading_expert_share - gate_second) * gates[..., 0] * gates[..., 1]
    logit_grad = (choose_first - choose_second) * logit_delta[..., None]
    gate_weight_grad = jnp.einsum(
        "bld,ble->de", acts_two.astype(jnp.float32), logit_grad, precision=exact_mode
    )
    acts_grad = jnp.einsum(
        "ble,de->bld", logit_grad, w_gate.astype(jnp.float32), precision=exact_mode
    )
    weighted_sel = first_sel * gates[..., 0:1, None] + runner_up_mask * gates[..., 1:2, None]
    slot_grad = jnp.einsum("blec,bld->ebcd", weighted_sel, gradient, precision=exact_mode)
    slot_grad = slot_grad.astype(jnp.bfloat16).reshape(EXPERTS, seq_count * CAP, model_width)
    owned_grad = lax.all_to_all(slot_grad, "exp", split_axis=0, concat_axis=1, tiled=True)
    grad_in = lax.all_gather(owned_grad, "seq", axis=1, tiled=True)
    hidden_grad = jnp.einsum(
        "erd,efd->erf", grad_in, second_weight, preferred_element_type=jnp.float32
    )
    _, gelu_pullback = jax.vjp(lambda values: jax.nn.gelu(values, approximate=False), pre_act)
    pre_grad = gelu_pullback(hidden_grad)[0].astype(jnp.bfloat16)
    second_grad = jnp.einsum("erf,erd->efd", hidden, grad_in, preferred_element_type=jnp.float32)
    first_grad = jnp.einsum("erd,erf->edf", expert_in, pre_grad, preferred_element_type=jnp.float32)
    input_part = jnp.einsum(
        "erf,edf->erd", pre_grad, first_weight, preferred_element_type=jnp.float32
    )
    input_grad = lax.psum_scatter(
        input_part.astype(jnp.bfloat16), "seq", scatter_dimension=1, tiled=True
    )
    local_count = w_in.shape[0]
    keep_local = (
        1 - lax.dynamic_slice_in_dim(frozen, lax.axis_index("exp") * local_count, local_count)
    ).astype(jnp.float32)
    first_grad = first_grad * keep_local[:, None, None]
    second_grad = second_grad * keep_local[:, None, None]
    routed_grad = lax.all_to_all(input_grad, "exp", split_axis=1, concat_axis=0, tiled=True)
    routed_grad = routed_grad.reshape(EXPERTS, seq_count, CAP, model_width).astype(jnp.float32)
    acts_grad = acts_grad + jnp.einsum(
        "blec,ebcd->bld", either_sel, routed_grad, precision=exact_mode
    )
    norm_two_grad, gain_second_grad = norm_backward(acts_grad, gain_second, unit_two, scale_two)
    mid_grad = gradient + norm_two_grad
    branch_grad = mid_grad.astype(jnp.bfloat16)
    out_weight_grad = jnp.einsum(
        "bld,ble->de", attended, branch_grad, preferred_element_type=jnp.float32
    )
    attended_grad = jnp.einsum(
        "ble,de->bld", branch_grad, w_o, preferred_element_type=jnp.float32
    ).astype(jnp.bfloat16)
    head_grads = lax.map(
        lambda operands: head_backward(operands, allowed),
        (
            query_heads,
            split_heads(gathered[0]),
            split_heads(gathered[1]),
            split_heads(attended_grad),
            log_total,
        ),
    )
    query_grad = merge_heads(head_grads[0]).astype(jnp.bfloat16)
    key_part = merge_heads(head_grads[1])
    value_part = merge_heads(head_grads[2])
    key_grad, value_grad = (
        lax.psum_scatter(
            key_part.astype(jnp.bfloat16), "seq", scatter_dimension=1, tiled=True
        ).astype(jnp.float32),
        lax.psum_scatter(
            value_part.astype(jnp.bfloat16), "seq", scatter_dimension=1, tiled=True
        ).astype(jnp.float32),
    )
    joined_grad = jnp.concatenate(
        [query_grad, key_grad.astype(jnp.bfloat16), value_grad.astype(jnp.bfloat16)], axis=-1
    )
    qkv_weight_grad = jnp.einsum(
        "bld,ble->de", acts_one, joined_grad, preferred_element_type=jnp.float32
    )
    acts_one_grad = jnp.einsum(
        "ble,de->bld", joined_grad, w_qkv, preferred_element_type=jnp.float32
    )
    norm_one_grad, gain_first_grad = norm_backward(acts_one_grad, gain_first, unit_one, scale_one)
    tokens_grad = mid_grad + norm_one_grad
    summed = lax.psum(
        (qkv_weight_grad, out_weight_grad, gate_weight_grad, gain_first_grad, gain_second_grad),
        ("seq", "exp"),
    )
    gate_keep = (1 - frozen).astype(jnp.float32)
    return (
        result.astype(jnp.bfloat16),
        tokens_grad,
        summed[3],
        summed[0],
        summed[1],
        summed[4],
        summed[2] * gate_keep[None, :],
        first_grad,
        second_grad,
    )


def solution(mesh):
    in_specs = (
        P("exp", "seq", None),
        P("exp", "seq", None),
        P(),
        P(),
        P(),
        P(),
        P(),
        P("exp", None, "seq"),
        P("exp", "seq", None),
        P("exp", "seq", None),
        P(),
    )
    out_specs = (
        P("exp", "seq", None),
        P("exp", "seq", None),
        P(),
        P(),
        P(),
        P(),
        P(),
        P("exp", None, "seq"),
        P("exp", "seq", None),
    )
    return jax.shard_map(
        on_device, mesh=mesh, in_specs=in_specs, out_specs=out_specs, check_vma=False
    )
```

profile of v0, /device:TPU:1, one launch (start us, length us, event | category | flops | bytes accessed | tf_op | source)
XLA Modules:
  0.0 1441.7 jit_solution(15068347872114077698)
XLA Ops:
  33.7 45.4 %all-gather.5.cloned.1.call-done = bf16[1,2048,768]{2,1,0:T(8,128)(2,1)} async-done(((bf16[1,256,768]{2,1,0:T(8,128)(2,1)}), bf16[1,2048,768]{2,1,0:T(8,128)(2,1)}) %all-gather.5.cloned.1.call-update) | async-done | bytes 3145744 | tf_op jit(solution)/shard_map/all_gather | solution.py:112
  83.9 6.5 copy.108
  90.4 53.0 %all-gather.7.cloned.1.call-done = bf16[1,2048,768]{2,1,0:T(8,128)(2,1)} async-done(((bf16[1,256,768]{2,1,0:T(8,128)(2,1)}), bf16[1,2048,768]{2,1,0:T(8,128)(2,1)}) %all-gather.7.cloned.1.call-update) | async-done | bytes 3145744 | tf_op jit(solution)/shard_map/all_gather | solution.py:113
  148.1 6.5 copy.109
  155.5 59.0 %while.28 = (s32[]{:T(128)}, bf16[12,1,256,64]{2,3,1,0:T(8,128)(2,1)}, f32[12,1,256]{2,1,0:T(1,128)}, bf16[12,1,256,64]{3,2,1,0:T(8,128)(2,1)}, bf16[12,1,2048,6...) while((s32[]{:T(128)}, ...), condition=%wide.region_5.6_spmd.clone, body=%wide.region_2.5_spmd.clone.sunk | while | flops 138936064 | bytes 7485013 | solution.py:116
  218.6 26.4 %all_to_all.66 = bf16[32,32,768]{2,1,0:T(8,128)(2,1)S(1)} all-to-all(bf16[32,32,768]{2,1,0:T(8,128)(2,1)S(1)} %convert_bitcast_fusion), channel_id=1, replica_groups=mesh['seq'=8,'exp'=16] {'exp'}, dimensions={0} | all-to-all | bytes 3145728 | tf_op jit(solution)/shard_map/all_to_all | solution.py:153
  251.0 27.5 %all_to_all.67 = bf16[32,32,768]{2,1,0:T(8,128)(2,1)S(1)} all-to-all(bf16[32,32,768]{2,1,0:T(8,128)(2,1)S(1)} %convolution_convert_fusion.3), channel_id=1, replica_groups=mesh['seq'=8,'exp'=16] {'exp'}, dimensions={0} | all-to-all | bytes 3145728 | tf_op jit(solution)/shard_map/all_to_all | solution.py:186
  280.1 126.2 %all-gather.9.cloned.1.call-done = bf16[2,4096,768]{2,1,0:T(8,128)(2,1)} async-done(((bf16[2,512,768]{2,1,0:T(8,128)(2,1)}), bf16[2,4096,768]{2,1,0:T(8,128)(2,1)}) %all-gather.9.cloned.1.call-update) | async-done | bytes 12582928 | tf_op jit(solution)/shard_map/all_gather | solution.py:154
  406.4 18.0 %fusion.52 = (u8[4096,384]{1,0:T(8,128)(4,1)}, u8[4096,384]{1,0:T(8,128)(4,1)}, f32[2,4096,384]{2,1,0:T(8,128)}) fusion(bf16[2,4096,768]{2,1,0:T(8,128)(2,1)} %all-gather.9.cloned.1.call-done, bf16[2,768,384]{2,1,0:T(8,128)(2,1)} %param.22), kind=kOutput, calls=%fused_computation.83 | convolution fusion | flops 4869586944 | bytes 29491200 | tf_op jit(solution)/shard_map/erd,edf->erf/dot_general | solution.py:156
  424.3 129.9 %all-gather.11.cloned.1.call-done = bf16[2,4096,768]{2,1,0:T(8,128)(2,1)} async-done(((bf16[2,512,768]{2,1,0:T(8,128)(2,1)}), bf16[2,4096,768]{2,1,0:T(8,128)(2,1)}) %all-gather.11.cloned.1.call-update) | async-done | bytes 12582928 | tf_op jit(solution)/shard_map/all_gather | solution.py:187
  554.2 38.9 %add_convert_fusion = (bf16[2,4096,384]{2,1,0:T(8,128)(2,1)}, f32[2,4096,384]{2,1,0:T(8,128)S(1)}) fusion(f32[2,4096,384]{2,1,0:T(8,128)} %get-tuple-element.281, u8[4096,384]{1,0:T(8,128)(4,1)} %get-tuple-element.215, u8[4096,384]{1,0:T(8,128)(4,1)} %get-tuple-element.214, bf16[2,4096,768]{2,1,0:T(8,128)(2,1)} %all-gather.11.cloned.1.call-done, ...), kind=kOutput, calls=%fused_computation.64 | convolution fusion | flops 5074059264 | bytes 48365568 | tf_op jit(solution)/shard_map/erd,efd->erf/dot_general | solution.py:188
  596.9 12.4 convolution_convert_fusion.1
  609.4 11.9 convolution_convert_fusion
  621.3 137.4 %reduce-scatter.5.cloned.1.call-done = bf16[2,512,768]{2,1,0:T(8,128)(2,1)} async-done(((bf16[2,4096,768]{2,1,0:T(8,128)(2,1)}), bf16[2,512,768]{2,1,0:T(8,128)(2,1)}) %reduce-scatter.5.cloned.1.call-update) | async-done | bytes 1572880 | tf_op jit(solution)/shard_map/reduce_scatter | solution.py:163
  768.5 157.5 %reduce-scatter.7.cloned.1.call-done = bf16[2,512,768]{2,1,0:T(8,128)(2,1)} async-done(((bf16[2,4096,768]{2,1,0:T(8,128)(2,1)}), bf16[2,512,768]{2,1,0:T(8,128)(2,1)}) %reduce-scatter.7.cloned.1.call-update) | async-done | bytes 1572880 | tf_op jit(solution)/shard_map/reduce_scatter | solution.py:198
  949.7 7.6 all-to-all-done.3
  976.2 120.0 %while.29 = (s32[]{:T(128)}, bf16[12,1,256,64]{2,3,1,0:T(8,128)(2,1)}, bf16[12,1,2048,64]{2,3,1,0:T(8,128)(2,1)}, bf16[12,1,2048,64]{2,3,1,0:T(8,128)(2,1)}, bf1...) while((s32[]{:T(128)}, ...), condition=%wide.region_22.23_spmd.clone, body=%wide.region_20.22_spmd.clone.sunk | while | flops 340934400 | bytes 18623600 | solution.py:221
  1105.0 66.7 %reduce-scatter.11.cloned.1.call-done = bf16[1,256,768]{1,2,0:T(8,128)(2,1)} async-done(((bf16[1,2048,768]{1,2,0:T(8,128)(2,1)}), bf16[1,256,768]{1,2,0:T(8,128)(2,1)}) %reduce-scatter.11.cloned.1.call-update) | async-done | bytes 393232 | tf_op jit(solution)/shard_map/reduce_scatter | solution.py:238
  1171.7 83.0 %reduce-scatter.9.cloned.1.call-done = bf16[1,256,768]{1,2,0:T(8,128)(2,1)} async-done(((bf16[1,2048,768]{1,2,0:T(8,128)(2,1)}), bf16[1,256,768]{1,2,0:T(8,128)(2,1)}) %reduce-scatter.9.cloned.1.call-update) | async-done | bytes 393232 | tf_op jit(solution)/shard_map/reduce_scatter | solution.py:235
  1261.0 12.7 convolution_multiply_fusion.5
  1273.7 13.5 convolution_multiply_fusion.4
  1289.9 66.1 %all-reduce = (f32[768]{0:T(1024)}, f32[768]{0:T(1024)}) all-reduce(f32[768]{0:T(1024)} %get-tuple-element.218, f32[768]{0:T(1024)S(1)} %copy-done.38), channel_id=1, replica_groups=mesh['seq'=8,'exp'=16] {'seq','exp'}, use_global_device_ids=true, to_apply=%region_28.29 | all-reduce | flops 1536 | bytes 12288 | tf_op jit(solution)/shard_map/psum | solution.py:253
  1360.6 64.6 %all-reduce.4.cloned.1.call-done = (f32[768,2304]{1,0:T(8,128)}, f32[768,768]{1,0:T(8,128)}, f32[768,32]{0,1:T(8,128)}) async-done(((f32[768,2304]{1,0:T(8,128)}, f32[768,768]{1,0:T(8,128)}, f32[768,32]{0,1:T(8,128)}), (f32[768,2304]{1,0:T(8,128)}, f32[768,768]{1,0:T(8,128)}, f32[768,32]{0,1:T(8,128)})) %all-reduce.4.cloned.1.call-update) | async-done | bytes 9535504 | tf_op jit(solution)/shard_map/psum | solution.py:253
  1426.8 6.6 copy.165
  (353 shorter events, 308.1 us)
Async XLA Ops:
  7.2 71.9 %all-gather.5.cloned.1.call-start = ((), (), s32[]{:S(2)}) async-start(), calls=%async_computation.8 | async-start | bytes 3538944 | tf_op jit(solution)/shard_map/all_gather | solution.py:112
  13.0 130.4 %all-gather.7.cloned.1.call-start = ((), (), s32[]{:S(2)}) async-start(), calls=%async_computation.9 | async-start | bytes 3538944 | tf_op jit(solution)/shard_map/all_gather | solution.py:113
  13.8 392.6 %all-gather.9.cloned.1.call-start = ((), (), s32[]{:S(2)}) async-start(), calls=%async_computation.10 | async-start | bytes 14155776 | tf_op jit(solution)/shard_map/all_gather | solution.py:154
  31.1 59.3 %copy-start.17 = (s32[32,32]{1,0:T(8,128)}, s32[32,32]{1,0:T(8,128)S(1)}, u32[]{:S(2)}) copy-start(s32[32,32]{1,0:T(8,128)S(1)} %multiply_add_fusion) | copy-start | bytes 12292
  155.4 62.0 %copy-start.19 = (f32[768]{0:T(1024)S(1)}, f32[768]{0:T(1024)}, u32[]{:S(2)}) copy-start(f32[768]{0:T(1024)} %param.20) | copy-start | bytes 9220
  155.4 62.2 %copy-start.22 = (s32[1024]{0:T(1024)S(1)}, s32[1024]{0:T(1024)}, u32[]{:S(2)}) copy-start(s32[1024]{0:T(1024)} %eq.255) | copy-start | bytes 12292
  155.5 62.2 %copy-start.43 = (s32[1,256,1]{1,2,0:T(1,128)S(1)}, s32[1,256,1]{1,2,0:T(1,128)}, u32[]{:S(2)}) copy-start(s32[1,256,1]{1,2,0:T(1,128)} %get-tuple-element.273) | copy-start | bytes 3076
  155.5 62.2 %copy-start.45 = (s32[1,256,1]{1,2,0:T(1,128)S(1)}, s32[1,256,1]{1,2,0:T(1,128)}, u32[]{:S(2)}) copy-start(s32[1,256,1]{1,2,0:T(1,128)} %get-tuple-element.274) | copy-start | bytes 3076
  218.4 27.9 %copy-start.27 = (s32[1,256,2]{1,2,0:T(2,128)S(1)}, s32[1,256,2]{1,2,0:T(2,128)}, u32[]{:S(2)}) copy-start(s32[1,256,2]{1,2,0:T(2,128)} %param.24) | copy-start | bytes 6148
  246.3 307.9 %all-gather.11.cloned.1.call-start = ((), (), s32[]{:S(2)}) async-start(), calls=%async_computation.12 | async-start | bytes 14155776 | tf_op jit(solution)/shard_map/all_gather | solution.py:187
  279.9 478.9 %reduce-scatter.5.cloned.1.call-start = ((), (), s32[]{:S(2)}) async-start(), calls=%async_computation.11 | async-start | bytes 14155776 | tf_op jit(solution)/shard_map/reduce_scatter | solution.py:163
  554.2 38.9 %copy-start.5 = (f32[2,4096,384]{2,1,0:T(8,128)S(1)}, f32[2,4096,384]{2,1,0:T(8,128)}, u32[]{:S(2)}) copy-start(f32[2,4096,384]{2,1,0:T(8,128)} %get-tuple-element.281) | copy-start | bytes 37748740
  609.3 316.6 %reduce-scatter.7.cloned.1.call-start = ((), (), s32[]{:S(2)}) async-start(), calls=%async_computation.13 | async-start | bytes 14155776 | tf_op jit(solution)/shard_map/reduce_scatter | solution.py:198
  621.3 314.5 %copy-start.18 = (s32[32,32]{1,0:T(8,128)S(1)}, s32[32,32]{1,0:T(8,128)}, u32[]{:S(2)}) copy-start(s32[32,32]{1,0:T(8,128)} %copy-done.17) | copy-start | bytes 12292
  762.9 167.2 %all-to-all-start.1 = ((bf16[2,512,768]{2,0,1:T(2,128)(2,1)}), bf16[2,512,768]{2,0,1:T(2,128)(2,1)}, u32[]{:S(2)}, u32[]{:S(2)}) async-start(bf16[2,512,768]{2,0,1:T(2,128)(2,1)} %copy.117), calls=%async_computation.2 | async-start | bytes 3145728 | tf_op jit(solution)/shard_map/all_to_all | solution.py:166
  930.1 27.2 %all-to-all-start.3 = ((bf16[2,512,768]{2,0,1:T(2,128)(2,1)}), bf16[2,512,768]{2,0,1:T(2,128)(2,1)}, u32[]{:S(2)}, u32[]{:S(2)}) async-start(bf16[2,512,768]{2,0,1:T(2,128)(2,1)} %copy.120), calls=%async_computation.5 | async-start | bytes 3145728 | tf_op jit(solution)/shard_map/all_to_all | solution.py:207
  935.7 236.0 %reduce-scatter.11.cloned.1.call-start = ((), (), s32[]{:S(2)}) async-start(), calls=%async_computation.15 | async-start | bytes 3538944 | tf_op jit(solution)/shard_map/reduce_scatter | solution.py:238
  949.7 16.5 %copy-start.44 = (s32[1,256,1]{1,2,0:T(1,128)S(1)}, s32[1,256,1]{1,2,0:T(1,128)}, u32[]{:S(2)}) copy-start(s32[1,256,1]{1,2,0:T(1,128)} %get-tuple-element.273) | copy-start | bytes 3076
  949.7 19.8 %copy-start.42 = (f32[1,256,1]{1,2,0:T(1,128)}, f32[1,256,1]{1,2,0:T(1,128)S(1)}, u32[]{:S(2)}) copy-start(f32[1,256,1]{1,2,0:T(1,128)S(1)} %multiply_multiply_fusion.5) | copy-start | bytes 3076
  1096.2 158.5 %copy-start.21 = (f32[768]{0:T(1024)S(1)}, f32[768]{0:T(1024)}, u32[]{:S(2)}) copy-start(f32[768]{0:T(1024)} %param.17) | copy-start | bytes 9220
  1096.2 158.5 %copy-start.31 = (f32[256]{0:T(256)S(1)}, f32[256]{0:T(256)}, u32[]{:S(2)}) copy-start(f32[256]{0:T(256)} %copy-done.30) | copy-start | bytes 3076
  1096.3 158.4 %reduce-scatter.9.cloned.1.call-start = ((), (), s32[]{:S(2)}) async-start(), calls=%async_computation.14 | async-start | bytes 3538944 | tf_op jit(solution)/shard_map/reduce_scatter | solution.py:235
  1097.0 328.2 %all-reduce.4.cloned.1.call-start = ((), (), s32[]{:S(2)}) async-start(), calls=%async_computation.16 | async-start | bytes 19070976 | tf_op jit(solution)/shard_map/psum | solution.py:253
  1273.7 13.6 copy-start.15
  (40 other events, 165.7 us)
Sparse Core Ops, SparseCore 0:
  13.2 65.8 all-gather.4
  82.0 61.3 all-gather.6
  246.4 159.8 all-gather.8
  409.0 145.1 all-gather.10
  609.4 149.2 reduce-scatter.4
  763.0 162.9 reduce-scatter.6
  1096.4 75.2 reduce-scatter.10
  1176.1 78.5 reduce-scatter.8
  1260.8 164.3 all-reduce.3
where the time goes:
time: 1450 us; the launch traced here: 1440 us
  waiting for transfers between devices  873 us (60%)
  matrix products  295 us (20%)
  blocking collectives  120 us (8%)
  local copies, waits for them, and re-layouts  96.4 us (7%)
  other arithmetic  30.3 us (2%)
  between operations  15 us (1%)
    reduce_scatter x1, waiting for transfers between devices, on_device(): lax.psum_scatter(input_part.astype(jnp.bfloat16), 'seq', scatter_dimensio...  157 us
    reduce_scatter x1, waiting for transfers between devices, on_device(): lax.psum_scatter(partial_out.astype(jnp.bfloat16), 'seq', scatter_dimensi...  137 us
    all_gather x1, waiting for transfers between devices, on_device(): grad_in = lax.all_gather(owned_grad, 'seq', axis=1, tiled=True)  130 us
    all_gather x1, waiting for transfers between devices, on_device(): expert_in = lax.all_gather(owned, 'seq', axis=1, tiled=True)  126 us
    reduce_scatter x1, waiting for transfers between devices, on_device(): lax.psum_scatter(key_part.astype(jnp.bfloat16), 'seq', scatter_dimension=...  83 us
    reduce_scatter x1, waiting for transfers between devices, on_device(): lax.psum_scatter(value_part.astype(jnp.bfloat16), 'seq', scatter_dimensio...  66.7 us
    psum x1, blocking collectives, on_device(): lax.psum((qkv_weight_grad, out_weight_grad, gate_weight_grad, gain_first_...  66.1 us
    psum x1, waiting for transfers between devices, on_device(): lax.psum((qkv_weight_grad, out_weight_grad, gate_weight_grad, gain_first_...  64.6 us
  transfers between devices with their start and end apart: 11, of which 10 were waited for; matrix products, arithmetic and copies ran while one was open for 9% of the time, Pallas kernels for 0%

commit v1 on v0

v1 whole, which is shorter than its diff:
```python
import functools
import math

import jax
import jax.numpy as jnp
from jax import lax
from jax.experimental import pallas as pl
from jax.experimental.pallas import tpu as pltpu
from jax.sharding import Mesh
from jax.sharding import PartitionSpec as P

D = 768
HEADS = 12
HEAD_DIM = 64
EXPERTS = 32
CAP = 32
ROWS = 256
BLOCKS = 8
FF = 3072
SLOTS = EXPERTS * CAP
EXTRA = 128
EPS = 1e-5
SCALE = HEAD_DIM ** -0.5
LOG2E = math.log2(math.e)
BF16 = jnp.bfloat16
F32 = jnp.float32
NEG = -1e30

SEQ = ("zh", "x")
GROUP = ("zh", "zl", "y", "c")
ALL = ("zh", "x", "zl", "y", "c")


def dot(a, b, ca=1, cb=0):
    return lax.dot_general(a, b, (((ca,), (cb,)), ((), ())), preferred_element_type=F32)


def params(mb=56):
    return pltpu.CompilerParams(vmem_limit_bytes=mb * 2**20)


def vspec(n):
    return [pl.BlockSpec(memory_space=pltpu.VMEM)] * n


def call(body, outs, n_in, scratch=(), **kw):
    return pl.pallas_call(
        body,
        out_shape=[jax.ShapeDtypeStruct(s, t) for s, t in outs],
        in_specs=vspec(n_in),
        out_specs=vspec(len(outs)),
        scratch_shapes=list(scratch),
        compiler_params=params(),
        **kw,
    )


def norm(v):
    mean = jnp.mean(v, axis=-1, keepdims=True)
    centred = v - mean
    inv = lax.rsqrt(jnp.mean(centred * centred, axis=-1, keepdims=True) + EPS)
    return centred * inv, inv


def norm_back(grad, gain, unit, inv):
    t = grad * gain
    m1 = jnp.mean(t, axis=-1, keepdims=True)
    m2 = jnp.mean(t * unit, axis=-1, keepdims=True)
    return inv * (t - m1 - unit * m2)


def lane_low():
    return lax.broadcasted_iota(jnp.int32, (1, 128), 1) < 64


def pair_up(wide, s):
    low = wide[:, 128 * (s // 2) : 128 * (s // 2) + 128]
    if s % 2:
        low = pltpu.roll(low, 64, 1)
    high = wide[:, 512 + 128 * (s // 4) : 640 + 128 * (s // 4)]
    if (s // 2) % 2 == 0:
        high = pltpu.roll(high, 64, 1)
    return jnp.where(lane_low(), low, high)


def unpair(tiles):
    out = []
    for t in range(4):
        out.append(
            jnp.where(lane_low(), tiles[2 * t], pltpu.roll(tiles[2 * t + 1], 64, 1))
        )
    for t in range(2):
        a = tiles[4 * t] + tiles[4 * t + 1]
        b = tiles[4 * t + 2] + tiles[4 * t + 3]
        out.append(jnp.where(lane_low(), pltpu.roll(a, 64, 1), b))
    return out


def project_body(tok_ref, gain_ref, w_ref, send_ref):
    unit, _ = norm(tok_ref[...].astype(F32))
    a1 = (unit * gain_ref[...]).astype(BF16)
    for part in range(3):
        wide = dot(a1, w_ref[:, part * D : part * D + D])
        for s in range(BLOCKS):
            send_ref[s, :, part * 128 : part * 128 + 128] = pair_up(wide, s).astype(
                BF16
            )


def unit_list(half):
    units = [(0, i, i + 1, i, i) for i in range(BLOCKS)]
    firsts = [(0, 1), (3, 2), (4, 5), (7, 6)]
    for t, (a, b) in enumerate(firsts):
        units.append((1, a + half * (b - a), 2 * t + 2, 2 * t, BLOCKS + t))
    return units


def masked_scores(k, q, block, first, count):
    s = dot(k, q, 1, 1)
    start = first * ROWS
    tail = (count - first) * ROWS
    keys = lax.broadcasted_iota(jnp.int32, (tail, ROWS), 0) + start
    queries = lax.broadcasted_iota(jnp.int32, (tail, ROWS), 1) + block * ROWS
    end = jnp.where(keys <= queries, s[start:], NEG)
    return end if start == 0 else jnp.concatenate([s[:start], end], axis=0)


def head_mask(h):
    low = lane_low()
    return (low if h == 0 else jnp.logical_not(low)).astype(F32).astype(BF16)


def attend_forward(half, qkv_ref, o_ref, ot_ref, lse_ref, vt_ref):
    c = SCALE * LOG2E
    for b in range(BLOCKS):
        vt_ref[:, b * ROWS : (b + 1) * ROWS] = qkv_ref[b, :, 256:384].T
        o_ref[b] = jnp.zeros((ROWS, 128), BF16)
    for h, block, count, first, u in unit_list(half):
        q = qkv_ref[block, :, 0:128] * head_mask(h)
        k = qkv_ref[0:count, :, 128:256].reshape(count * ROWS, 128)
        s = masked_scores(k, q, block, first, count)
        top = jnp.max(s, axis=0, keepdims=True)
        p = jnp.exp2((s - top) * c)
        total = jnp.sum(p, axis=0, keepdims=True)
        ot = dot(vt_ref[64 * h : 64 * h + 64, 0 : count * ROWS], p.astype(BF16))
        ot = ot / total
        ot_ref[u] = ot
        lse_ref[u] = jnp.broadcast_to(top * c + jnp.log2(total), (8, ROWS))
        wide = jnp.concatenate([ot, jnp.zeros_like(ot)] if h == 0 else [jnp.zeros_like(ot), ot], axis=0)
        o_ref[block] = (o_ref[block].astype(F32) + wide.T).astype(BF16)


def attend_backward(half, qkv_ref, do_ref, ot_ref, lse_ref, out_ref, kt_ref, dk_ref, dv_ref):
    c = SCALE * LOG2E
    for b in range(BLOCKS):
        kt_ref[:, b * ROWS : (b + 1) * ROWS] = qkv_ref[b, :, 128:256].T
        out_ref[b, :, 0:128] = jnp.zeros((ROWS, 128), BF16)
    dk_ref[...] = jnp.zeros_like(dk_ref)
    dv_ref[...] = jnp.zeros_like(dv_ref)
    for h, block, count, first, u in unit_list(half):
        rows = count * ROWS
        q = qkv_ref[block, :, 0:128] * head_mask(h)
        do = do_ref[block] * head_mask(h)
        dot_rows = do.astype(F32).T[64 * h : 64 * h + 64]
        delta = jnp.sum(dot_rows * ot_ref[u], axis=0, keepdims=True)
        lse = lse_ref[u][0:1]
        k = qkv_ref[0:count, :, 128:256].reshape(rows, 128)
        v = qkv_ref[0:count, :, 256:384].reshape(rows, 128)
        s = masked_scores(k, q, block, first, count)
        p = jnp.exp2(s * c - lse)
        dp = dot(v, do, 1, 1)
        ds = (p * (dp - delta)).astype(BF16)
        dv_ref[0:rows] += dot(p.astype(BF16), do)
        dk_ref[0:rows] += dot(ds, q)
        dqt = dot(kt_ref[64 * h : 64 * h + 64, 0:rows], ds) * SCALE
        wide = jnp.concatenate([dqt, jnp.zeros_like(dqt)] if h == 0 else [jnp.zeros_like(dqt), dqt], axis=0)
        out_ref[block, :, 0:128] = (
            out_ref[block, :, 0:128].astype(F32) + wide.T
        ).astype(BF16)
    for b in range(BLOCKS):
        at = slice(b * ROWS, (b + 1) * ROWS)
        out_ref[b, :, 128:256] = (dk_ref[at] * SCALE).astype(BF16)
        out_ref[b, :, 256:384] = dv_ref[at].astype(BF16)


def half_of(index):
    return (index + index // 2) % 2


def choices(routes):
    ids = lax.broadcasted_iota(jnp.int32, (ROWS, EXPERTS), 1)
    e1, e2 = routes[:, 0:1], routes[:, 1:2]
    m1, m2 = (e1 == ids).astype(F32), (e2 == ids).astype(F32)
    r = lax.broadcasted_iota(jnp.int32, (ROWS, ROWS), 0)
    k = lax.broadcasted_iota(jnp.int32, (ROWS, ROWS), 1)
    lower = (k < r).astype(F32).astype(BF16)
    earlier = dot(lower, (m1 + m2).astype(BF16))
    s1 = jnp.sum(earlier * m1, axis=1, keepdims=True)
    s2 = jnp.sum(earlier * m2, axis=1, keepdims=True)

    def column(e, s):
        place = (e % 2) * (EXPERTS // 2) + e // 2
        return (place * CAP).astype(F32) + s

    return m1, m2, column(e1, s1), column(e2, s2)


def chosen(col):
    at = lax.broadcasted_iota(jnp.int32, (ROWS, SLOTS), 1).astype(F32)
    return (at == col).astype(F32).astype(BF16)


def chosen_t(col):
    row = jnp.broadcast_to(col, (ROWS, 128)).T[0:1]
    at = lax.broadcasted_iota(jnp.int32, (SLOTS, ROWS), 0).astype(F32)
    return (at == row).astype(F32).astype(BF16)


def two_parts(v):
    lane = lax.broadcasted_iota(jnp.int32, (v.shape[0], EXTRA), 1)
    high = v.astype(BF16).astype(F32)
    return jnp.where(lane == 0, high, jnp.where(lane == 1, v - high, 0.0)).astype(BF16)


def from_parts(v):
    lane = lax.broadcasted_iota(jnp.int32, v.shape, 1)
    return jnp.sum(jnp.where(lane < 2, v.astype(F32), 0.0), axis=1, keepdims=True)


def deal_body(cot_ref, routes_ref, send_ref):
    _, _, c1, c2 = choices(routes_ref[...])
    either = chosen_t(c1) + chosen_t(c2)
    send_ref[...] = dot(either, cot_ref[...]).astype(BF16)


def middle_body(o_ref, tok_ref, w_o_ref, gain_ref, gate_ref, routes_ref, mid_ref, att_ref, send_ref, gates_ref):
    tiles = unpair([o_ref[s].astype(F32) for s in range(BLOCKS)])
    o = jnp.concatenate([t.astype(BF16) for t in tiles], axis=1)
    att_ref[...] = o
    mid = tok_ref[...].astype(F32) + dot(o, w_o_ref[...])
    mid_ref[...] = mid
    unit, _ = norm(mid)
    a2 = (unit * gain_ref[...]).astype(BF16)
    logits = dot(a2, gate_ref[...])
    m1, m2, c1, c2 = choices(routes_ref[...])
    l1 = jnp.sum(logits * m1, axis=1, keepdims=True)
    l2 = jnp.sum(logits * m2, axis=1, keepdims=True)
    top = jnp.maximum(l1, l2)
    x1, x2 = jnp.exp(l1 - top), jnp.exp(l2 - top)
    g1, g2 = x1 / (x1 + x2), x2 / (x1 + x2)
    lane = lax.broadcasted_iota(jnp.int32, (ROWS, 128), 1)
    gates_ref[...] = jnp.where(lane == 0, g1, g2)
    t1, t2 = chosen_t(c1), chosen_t(c2)
    send_ref[:, 0:D] = dot(t1 + t2, a2).astype(BF16)
    send_ref[:, D:] = (dot(t1, two_parts(g1)) + dot(t2, two_parts(g2))).astype(BF16)


def erf_parts(h):
    x = jnp.abs(h) * (0.5**0.5)
    t = 1.0 / (1.0 + 0.3275911 * x)
    e = jnp.exp(-0.5 * h * h)
    poly = t * (
        0.254829592
        + t * (-0.284496736 + t * (1.421413741 + t * (-1.453152027 + t * 1.061405429)))
    )
    tail = 0.5 * poly * e
    return jnp.where(h >= 0, 1.0 - tail, tail), e * (1.0 / math.sqrt(2.0 * math.pi))


STEP = 256


def expert_body(x_ref, c_ref, win_ref, wout_ref, ret_ref, y_ref, dwin_ref, dwout_ref, g_ref, dh_ref, dx_ref, ya_ref, dg_ref, xg_ref, cg_ref):
    i = pl.program_id(0)
    n = pl.num_programs(0)

    @pl.when(i == 0)
    def _():
        dx_ref[...] = jnp.zeros_like(dx_ref)
        ya_ref[...] = jnp.zeros_like(ya_ref)
        dg_ref[...] = jnp.zeros_like(dg_ref)

    w_in, w_out = win_ref[0], wout_ref[0]

    def rows(r, carry):
        at = pl.ds(pl.multiple_of(r * STEP, STEP), STEP)
        gate = from_parts(x_ref[at, D:])
        x, c = x_ref[at, 0:D], c_ref[at, :]

        @pl.when(i == 0)
        def _():
            xg_ref[at, :] = x
            cg_ref[at, :] = (gate * c.astype(F32)).astype(BF16)

        h = dot(x, w_in)
        cw = dot(cg_ref[at, :], w_out, 1, 1)
        phi, density = erf_parts(h)
        g = (h * phi).astype(BF16)
        dh = ((phi + h * density) * cw).astype(BF16)
        g_ref[at, :] = g
        dh_ref[at, :] = dh
        back = dot(dh, w_in, 1, 1)
        out = dot(g, w_out)
        dx_ref[at, :] += back
        ya_ref[at, :] += out
        return carry

    lax.fori_loop(0, SLOTS // STEP, rows, 0)
    dwin_ref[0] = dot(xg_ref[...], dh_ref[...], 0, 0).astype(BF16)
    dwout_ref[0] = dot(g_ref[...], cg_ref[...], 0, 0).astype(BF16)

    @pl.when(i == n - 1)
    def _():
        def finish(r, carry):
            at = pl.ds(pl.multiple_of(r * STEP, STEP), STEP)
            y = ya_ref[at, :].astype(BF16)
            y_ref[at, :] = y
            dgate = jnp.sum(
                c_ref[at, :].astype(F32) * y.astype(F32), axis=1, keepdims=True
            )
            ret_ref[at, 0:D] = dx_ref[at, :].astype(BF16)
            ret_ref[at, D:] = two_parts(dgate)
            return carry

        lax.fori_loop(0, SLOTS // STEP, finish, 0)


def experts(x, c, w_in, w_out):
    n, _, width = w_in.shape
    whole = lambda shape: pl.BlockSpec(shape, lambda i: (0,) * len(shape))
    return pl.pallas_call(
        expert_body,
        grid=(n,),
        out_shape=[
            jax.ShapeDtypeStruct((SLOTS, D + EXTRA), BF16),
            jax.ShapeDtypeStruct((SLOTS, D), BF16),
            jax.ShapeDtypeStruct((n, D, width), BF16),
            jax.ShapeDtypeStruct((n, width, D), BF16),
        ],
        in_specs=[
            whole((SLOTS, D + EXTRA)),
            whole((SLOTS, D)),
            pl.BlockSpec((1, D, width), lambda i: (i, 0, 0)),
            pl.BlockSpec((1, width, D), lambda i: (i, 0, 0)),
        ],
        out_specs=[
            whole((SLOTS, D + EXTRA)),
            whole((SLOTS, D)),
            pl.BlockSpec((1, D, width), lambda i: (i, 0, 0)),
            pl.BlockSpec((1, width, D), lambda i: (i, 0, 0)),
        ],
        scratch_shapes=[
            pltpu.VMEM((SLOTS, width), BF16),
            pltpu.VMEM((SLOTS, width), BF16),
            pltpu.VMEM((SLOTS, D), F32),
            pltpu.VMEM((SLOTS, D), F32),
            pltpu.VMEM((SLOTS, 128), F32),
            pltpu.VMEM((SLOTS, D), BF16),
            pltpu.VMEM((SLOTS, D), BF16),
        ],
        compiler_params=params(60),
    )(x, c, w_in, w_out)


def back_body(ret_ref, cot_ref, routes_ref, gates_ref, mid_ref, att_ref, gain_ref, gate_w_ref, w_o_ref,
              send_ref, dmid_ref, o_grad_ref, gate_grad_ref, gain_grad_ref):
    m1, m2, c1, c2 = choices(routes_ref[...])
    s1, s2 = chosen(c1), chosen(c2)
    g1, g2 = gates_ref[:, 0:1], gates_ref[:, 1:2]
    extra = ret_ref[:, D:]
    d1, d2 = from_parts(dot(s1, extra)), from_parts(dot(s2, extra))
    dl = g1 * g2 * (d1 - d2)
    dlogits = (m1 - m2) * dl
    unit, inv = norm(mid_ref[...])
    a2 = (unit * gain_ref[...]).astype(BF16)
    high = dlogits.astype(BF16)
    low = (dlogits - high.astype(F32)).astype(BF16)
    gate_grad_ref[...] = dot(a2, high, 0, 0) + dot(a2, low, 0, 0)
    gate_w = gate_w_ref[...]
    da2 = dot(s1 + s2, ret_ref[:, 0:D]) + dot(high, gate_w, 1, 1) + dot(low, gate_w, 1, 1)
    gain_grad_ref[...] = jnp.sum(da2 * unit, axis=0, keepdims=True)
    dmid = cot_ref[...].astype(F32) + norm_back(da2, gain_ref[...], unit, inv)
    dmid_ref[...] = dmid
    datt = dmid.astype(BF16)
    o_grad_ref[...] = dot(att_ref[...], datt, 0, 0)
    do = dot(datt, w_o_ref[...], 1, 1)
    for s in range(BLOCKS):
        send_ref[s] = pair_up(do, s).astype(BF16)


def out_body(y_ref, mid_ref, gates_ref, routes_ref, out_ref):
    _, _, c1, c2 = choices(routes_ref[...])
    y = y_ref[...]
    mix = gates_ref[:, 0:1] * dot(chosen(c1), y) + gates_ref[:, 1:2] * dot(chosen(c2), y)
    out_ref[...] = (mid_ref[...] + mix).astype(BF16)


def finish_body(dqkv_ref, tok_ref, gain_ref, w_ref, dmid_ref, tok_grad_ref, qkv_grad_ref, gain_grad_ref):
    unit, inv = norm(tok_ref[...].astype(F32))
    a1 = (unit * gain_ref[...]).astype(BF16)
    da1 = jnp.zeros((ROWS, D), F32)
    for part in range(3):
        tiles = unpair(
            [dqkv_ref[s, :, part * 128 : part * 128 + 128].astype(F32) for s in range(BLOCKS)]
        )
        d = jnp.concatenate([t.astype(BF16) for t in tiles], axis=1)
        at = slice(part * D, part * D + D)
        qkv_grad_ref[:, at] = dot(a1, d, 0, 0)
        da1 = da1 + dot(d, w_ref[:, at], 1, 1)
    gain_grad_ref[...] = jnp.sum(da1 * unit, axis=0, keepdims=True)
    tok_grad_ref[...] = dmid_ref[...] + norm_back(da1, gain_ref[...], unit, inv)


def on_device(tokens, cotangent, gain_first, w_qkv, w_o, gain_second, w_gate, w_in, w_out, routes, frozen):
    zh = lax.axis_index("zh")
    s = zh * 4 + lax.axis_index("x")
    e = (lax.axis_index("zl") * 4 + lax.axis_index("y")) * 2 + lax.axis_index("c")
    half = s % 2
    tok, cot, routes = tokens[0], cotangent[0], routes[0]
    gain1, gain2 = gain_first.reshape(1, D), gain_second.reshape(1, D)

    swap = [(0, 1), (1, 0)]

    def gather(w, axis):
        own = lax.dynamic_index_in_dim(w, zh, 0, keepdims=False)
        other = lax.dynamic_index_in_dim(w, 1 - zh, 0, keepdims=False)
        got = lax.ppermute(other, "zh", swap)
        return lax.all_gather(jnp.concatenate([own, got], axis=axis), "x")

    w_in_full = gather(w_in, 1)
    w_out_full = gather(w_out, 0)

    c_send = call(deal_body, [((SLOTS, D), BF16)], 2)(cot, routes)[0]
    c_rows = lax.all_to_all(c_send.reshape(32, CAP, D), GROUP, 0, 0, tiled=True)

    qkv_send = call(project_body, [((BLOCKS, ROWS, 384), BF16)], 3)(tok, gain1, w_qkv)[0]
    qkv = lax.all_to_all(qkv_send, SEQ, 0, 0, tiled=True)

    def fwd(*refs):
        attend_forward(lax.axis_index("x") % 2, *refs)

    o_send, ot, lse = call(
        fwd,
        [((BLOCKS, ROWS, 128), BF16), ((12, 64, ROWS), F32), ((12, 8, ROWS), F32)],
        1,
        [pltpu.VMEM((128, BLOCKS * ROWS), BF16)],
    )(qkv)
    o = lax.all_to_all(o_send, SEQ, 0, 0, tiled=True)
    mid, att, x_send, gates = call(
        middle_body,
        [((ROWS, D), F32), ((ROWS, D), BF16), ((SLOTS, D + EXTRA), BF16), ((ROWS, 128), F32)],
        6,
    )(o, tok, w_o, gain2, w_gate, routes)
    x_rows = lax.all_to_all(x_send.reshape(32, CAP, D + EXTRA), GROUP, 0, 0, tiled=True)
    ret, y, dw_in, dw_out = experts(
        x_rows.reshape(SLOTS, D + EXTRA), c_rows.reshape(SLOTS, D), w_in_full, w_out_full
    )
    ret = lax.all_to_all(ret.reshape(32, CAP, D + EXTRA), GROUP, 0, 0, tiled=True).reshape(SLOTS, D + EXTRA)
    y = lax.all_to_all(y.reshape(32, CAP, D), GROUP, 0, 0, tiled=True).reshape(SLOTS, D)

    keep = (1 - lax.dynamic_slice_in_dim(frozen, 2 * e, 2)).astype(F32)

    def scatter(dw, axis):
        mine = lax.psum_scatter(dw, "x", scatter_dimension=0, tiled=False)
        own, other = jnp.split(mine, 2, axis=axis)
        got = lax.ppermute(other, "zh", swap)
        first = jnp.where(zh == 0, own, got).astype(F32)
        second = jnp.where(zh == 0, got, own).astype(F32)
        return jnp.stack([first, second]) * keep[:, None, None]

    w_in_grad = scatter(dw_in, 1)
    w_out_grad = scatter(dw_out, 0)

    do_send, dmid, o_grad, gate_grad, gain2_grad = call(
        back_body,
        [((BLOCKS, ROWS, 128), BF16), ((ROWS, D), F32), ((D, D), F32), ((D, EXPERTS), F32), ((1, D), F32)],
        9,
    )(ret, cot, routes, gates, mid, att, gain2, w_gate, w_o)
    do = lax.all_to_all(do_send, SEQ, 0, 0, tiled=True)

    def bwd(*refs):
        attend_backward(lax.axis_index("x") % 2, *refs)

    dqkv_send = call(
        bwd,
        [((BLOCKS, ROWS, 384), BF16)],
        4,
        [
            pltpu.VMEM((128, BLOCKS * ROWS), BF16),
            pltpu.VMEM((BLOCKS * ROWS, 128), F32),
            pltpu.VMEM((BLOCKS * ROWS, 128), F32),
        ],
    )(qkv, do, ot, lse)[0]
    dqkv = lax.all_to_all(dqkv_send, SEQ, 0, 0, tiled=True)
    out = call(out_body, [((ROWS, D), BF16)], 4)(y, mid, gates, routes)[0]
    tok_grad, qkv_grad, gain1_grad = call(
        finish_body, [((ROWS, D), F32), ((D, 3 * D), F32), ((1, D), F32)], 5
    )(dqkv, tok, gain1, w_qkv, dmid)
    qkv_grad, o_grad, gate_grad, gain1_grad, gain2_grad = lax.psum(
        (qkv_grad, o_grad, gate_grad, gain1_grad, gain2_grad), ALL
    )
    return (
        out[None],
        tok_grad[None],
        gain1_grad.reshape(D),
        qkv_grad,
        o_grad,
        gain2_grad.reshape(D),
        gate_grad * (1 - frozen).astype(F32)[None, :],
        w_in_grad,
        w_out_grad,
    )


def solution(mesh):
    fine = Mesh(mesh.devices.reshape(2, 4, 2, 4, 2), ALL)
    seq, exp = ("zh", "x"), ("zl", "y", "c")
    in_specs = (
        P(exp, seq, None),
        P(exp, seq, None),
        P(),
        P(),
        P(),
        P(),
        P(),
        P(exp, None, seq),
        P(exp, seq, None),
        P(exp, seq, None),
        P(),
    )
    out_specs = (
        P(exp, seq, None),
        P(exp, seq, None),
        P(),
        P(),
        P(),
        P(),
        P(),
        P(exp, None, seq),
        P(exp, seq, None),
    )
    return jax.shard_map(on_device, mesh=fine, in_specs=in_specs, out_specs=out_specs, check_vma=False)
```

time: 1450 us -> 572 us (0.39)
  waiting for transfers between devices: 873 us -> 148 us
  matrix products: 295 us -> 0 us
  blocking collectives: 120 us -> 232 us
  Pallas kernels: 0 us -> 106 us
  local copies, waits for them, and re-layouts: 96.4 us -> 17.1 us
  starting transfers between devices: 12 us -> 36.2 us
  other arithmetic: 30.3 us -> 9.82 us
    reduce_scatter x4 -> x2, waiting for transfers between devices: 445 us -> 0.02 us  [scatter(): mine = lax.psum_scatter(dw, 'x', scatter_dimension=0, tiled=False)]
    all_gather x4 -> x2, waiting for transfers between devices: 355 us -> 0.01 us  [gather(): return lax.all_gather(jnp.concatenate([own, got], axis=axis), 'x')]
    dot_general x103 -> x0, matrix products: 294 us -> none  [the longest x1 38.9 us: on_device(): jnp.einsum('erd,efd->erf', grad_in, second_weight, preferred_element_type...]
    all_to_all x2 -> x5, blocking collectives: 53.9 us -> 163 us  [the longest x1 42.5 us: on_device(): qkv = lax.all_to_all(qkv_send, SEQ, 0, 0, tiled=True)]
    pallas_call x0 -> x9, Pallas kernels: none -> 106 us  [the longest x1 49.1 us: experts(): pl.pallas_call(expert_body, grid=(n,), out_shape=[jax.ShapeDtypeStruct((S...]
    all_to_all x2 -> x3, waiting for transfers between devices: 7.6 us -> 39.2 us  [the longest x1 18.6 us: on_device(): lax.all_to_all(y.reshape(32, CAP, D), GROUP, 0, 0, tiled=True)]
    ppermute x0 -> x4, waiting for transfers between devices: none -> 25.5 us  [the longest x2 25.5 us: gather(): got = lax.ppermute(other, 'zh', swap)]
    psum x1, waiting for transfers between devices: 64.6 us -> 82.3 us  [on_device(): lax.psum((qkv_grad, o_grad, gate_grad, gain1_grad, gain2_grad), ALL)]
  transfers between devices with their start and end apart: 11 -> 12, of which waited for: 10 -> 6; matrix products, arithmetic and copies ran while one was open for 9% -> 2% of each run, Pallas kernels for 0% -> 10%
where the time goes in v1:
time: 572 us; the launch traced here: 563 us
  blocking collectives  232 us (41%)
  waiting for transfers between devices  148 us (26%)
  Pallas kernels  106 us (19%)
  starting transfers between devices  36.2 us (6%)
  local copies, waits for them, and re-layouts  17.1 us (3%)
  between operations  14.4 us (3%)
  other arithmetic  9.82 us (2%)
    psum x1, waiting for transfers between devices, on_device(): lax.psum((qkv_grad, o_grad, gate_grad, gain1_grad, gain2_grad), ALL)  82.3 us
    psum x1, blocking collectives, on_device(): lax.psum((qkv_grad, o_grad, gate_grad, gain1_grad, gain2_grad), ALL)  68.7 us
    pallas_call x1, Pallas kernels, experts(): pl.pallas_call(expert_body, grid=(n,), out_shape=[jax.ShapeDtypeStruct((S...  49.1 us
    all_to_all x1, blocking collectives, on_device(): qkv = lax.all_to_all(qkv_send, SEQ, 0, 0, tiled=True)  42.5 us
    all_to_all x1, blocking collectives, on_device(): dqkv = lax.all_to_all(dqkv_send, SEQ, 0, 0, tiled=True)  41.3 us
    all_to_all x1, blocking collectives, on_device(): lax.all_to_all(x_send.reshape(32, CAP, D + EXTRA), GROUP, 0, 0, tiled=True)  31.9 us
    all_to_all x1, blocking collectives, on_device(): lax.all_to_all(ret.reshape(32, CAP, D + EXTRA), GROUP, 0, 0, tiled=True)  29.5 us
    ppermute x2, waiting for transfers between devices, gather(): got = lax.ppermute(other, 'zh', swap)  25.5 us
  transfers between devices with their start and end apart: 12, of which 6 were waited for; matrix products, arithmetic and copies ran while one was open for 2% of the time, Pallas kernels for 10%

profile of v1, /device:TPU:1, one launch (start us, length us, event | category | flops | bytes accessed | tf_op | source)
XLA Modules:
  0.0 563.1 jit_solution(17530419609920243059)
XLA Ops:
  8.6 4.5 collective-permute-start.1
  13.1 13.1 %collective-permute-done.1 = bf16[384,768]{1,0:T(8,128)(2,1)S(1)} collective-permute-done((bf16[384,768]{1,0:T(8,128)(2,1)S(1)}, bf16[384,768]{1,0:T(8,128)(2,1)S(1)}, u32[]{:S(2)}, u32[]{:S(2)}) %collective-permute-start.1) | collective-permute-done | bytes 589856 | tf_op jit(solution)/shard_map/ppermute | solution.py:427
  30.7 12.5 %collective-permute-done = bf16[768,384]{1,0:T(8,128)(2,1)S(1)} collective-permute-done((bf16[768,384]{1,0:T(8,128)(2,1)S(1)}, bf16[768,384]{1,0:T(8,128)(2,1)S(1)}, u32[]{:S(2)}, u32[]{:S(2)}) %collective-permute-start) | collective-permute-done | bytes 589856 | tf_op jit(solution)/shard_map/ppermute | solution.py:427
  44.8 4.7 shard_map.178
  49.5 42.5 %all_to_all.40.refs_0_ = bf16[8,256,384]{2,1,0:T(8,128)(2,1)} all-to-all(bf16[8,256,384]{2,1,0:T(8,128)(2,1)} %shard_map.178), channel_id=1, replica_groups=mesh['zh'=2,'x'=4,'zl'=2,'y'=4,'c'=2] {'zh','x'}, dimensions={0} | all-to-all | bytes 3145728 | tf_op jit(solution)/shard_map/all_to_all | solution.py:437
  92.0 11.4 %shard_map.179 = (bf16[8,256,128]{2,1,0:T(8,128)(2,1)}, f32[12,64,256]{2,1,0:T(8,128)}, f32[12,8,256]{2,1,0:T(8,128)}) custom-call(bf16[8,256,384]{2,1,0:T(8,128)(2,1)} %all_to_all.40.refs_0_), custom_call_target="tpu_custom_call" | custom-call | tf_op jit(solution)/shard_map/pallas_call | solution.py:442
  103.4 5.0 all-to-all-start.1
  112.6 4.9 all-to-all-done.1.o_ref
  118.3 12.9 %all-to-all-start.3 = ((bf16[32,32,768]{2,1,0:T(8,128)(2,1)}), bf16[32,32,768]{2,1,0:T(8,128)(2,1)S(1)}, u32[]{:S(2)}, u32[]{:S(2)}) async-start(bf16[32,32,768]{2,1,0:T(8,128)(2,1)} %bitcast.46), calls=%async_computation.3 | async-start | bytes 3145728 | tf_op jit(solution)/shard_map/all_to_all | solution.py:434
  132.7 5.0 shard_map.180
  137.7 15.7 %all-to-all-done.3 = bf16[32,32,768]{2,1,0:T(8,128)(2,1)S(1)} async-done(((bf16[32,32,768]{2,1,0:T(8,128)(2,1)}), bf16[32,32,768]{2,1,0:T(8,128)(2,1)S(1)}, u32[]{:S(2)}, u32[]{:S(2)}) %all-to-all-start.3) | async-done | bytes 1572896 | tf_op jit(solution)/shard_map/all_to_all | solution.py:434
  153.4 31.9 %all_to_all.41 = bf16[32,32,896]{2,1,0:T(8,128)(2,1)} all-to-all(bf16[32,32,896]{2,1,0:T(8,128)(2,1)} %bitcast.57), channel_id=1, replica_groups=mesh['zh'=2,'x'=4,'zl'=2,'y'=4,'c'=2] {'zh','zl','y','c'}, dimensions={0} | all-to-all | bytes 3670016 | tf_op jit(solution)/shard_map/all_to_all | solution.py:454
  185.3 49.1 %shard_map.182 = (bf16[1024,896]{1,0:T(8,128)(2,1)}, bf16[1024,768]{1,0:T(8,128)(2,1)}, bf16[4,768,768]{2,1,0:T(8,128)(2,1)}, bf16[4,768,768]{2,1,0:T(8,128)(2,1)}) custom-call(bf16[1024,896]{1,0:T(8,128)(2,1)} %bitcast.40, bf16[1024,768]{1,0:T(8,128)(2,1)} %bitcast.45, bf16[4,768,768]{2,1,0:T(8,128)(2,1)} %bitcast.48, bf16[4,768,768]{2,1,0:T(8,128)(2,1)} %bitcast.47), custom_call_target="tpu_custom_call" | custom-call | tf_op jit(solution)/shard_map/pallas_call | solution.py:331
  236.0 29.5 %all_to_all.42 = bf16[32,32,896]{2,1,0:T(8,128)(2,1)} all-to-all(bf16[32,32,896]{2,1,0:T(8,128)(2,1)S(1)} %bitcast.56), channel_id=1, replica_groups=mesh['zh'=2,'x'=4,'zl'=2,'y'=4,'c'=2] {'zh','zl','y','c'}, dimensions={0} | all-to-all | bytes 3670016 | tf_op jit(solution)/shard_map/all_to_all | solution.py:458
  265.5 7.7 %shard_map.184 = (bf16[8,256,128]{2,1,0:T(8,128)(2,1)}, f32[256,768]{1,0:T(8,128)}, f32[768,768]{1,0:T(8,128)}, f32[768,32]{1,0:T(8,128)}, f32[1,768]{1,0:T(1,128)}) custom-call(bf16[1024,896]{1,0:T(8,128)(2,1)} %bitcast.41, bf16[256,768]{1,0:T(8,128)(2,1)} %bitcast.59, s32[256,2]{1,0:T(8,128)} %bitcast.54, f32[256,128]{1,0:T(8,128)} %get-tuple-element.32.gates_ref, ...), custom_call_target="tpu_custom_call" | custom-call | tf_op jit(solution)/shard_map/pallas_call | solution.py:474
  273.2 18.2 %all_to_all.43.refs_1_ = bf16[8,256,128]{2,1,0:T(8,128)(2,1)} all-to-all(bf16[8,256,128]{2,1,0:T(8,128)(2,1)} %get-tuple-element.35), channel_id=1, replica_groups=mesh['zh'=2,'x'=4,'zl'=2,'y'=4,'c'=2] {'zh','x'}, dimensions={0} | all-to-all | bytes 1048576 | tf_op jit(solution)/shard_map/all_to_all | solution.py:479
  291.3 12.6 %shard_map.185 = bf16[8,256,384]{2,1,0:T(8,128)(2,1)} custom-call(bf16[8,256,384]{2,1,0:T(8,128)(2,1)} %all_to_all.40.refs_0_, bf16[8,256,128]{2,1,0:T(8,128)(2,1)} %all_to_all.43.refs_1_, f32[12,64,256]{2,1,0:T(8,128)} %get-tuple-element.36.refs_2_, f32[12,8,256]{2,1,0:T(8,128)} %get-tuple-element.37.refs_3_), custom_call_target="tpu_custom_call" | custom-call | tf_op jit(solution)/shard_map/pallas_call | solution.py:484
  303.9 41.3 %all_to_all.44.dqkv_ref = bf16[8,256,384]{2,1,0:T(8,128)(2,1)} all-to-all(bf16[8,256,384]{2,1,0:T(8,128)(2,1)} %shard_map.185), channel_id=1, replica_groups=mesh['zh'=2,'x'=4,'zl'=2,'y'=4,'c'=2] {'zh','x'}, dimensions={0} | all-to-all | bytes 3145728 | tf_op jit(solution)/shard_map/all_to_all | solution.py:494
  345.2 8.3 %shard_map.186 = (f32[256,768]{1,0:T(8,128)}, f32[768,2304]{1,0:T(8,128)}, f32[1,768]{1,0:T(1,128)}) custom-call(bf16[8,256,384]{2,1,0:T(8,128)(2,1)} %all_to_all.44.dqkv_ref, bf16[256,768]{1,0:T(8,128)(2,1)} %bitcast.51, f32[1,768]{1,0:T(1,128)} %reshape.58.gain_ref, bf16[768,2304]{1,0:T(8,128)(2,1)} %w_ref.3, f32[256,768]{1,0:T(8,128)} %get-tuple-element.38.dmid_ref), custom_call_target="tpu_custom_call" | custom-call | tf_op jit(solution)/shard_map/pallas_call | solution.py:496
  353.5 6.3 %all-to-all-start.4 = ((bf16[32,32,768]{2,1,0:T(8,128)(2,1)}), bf16[32,32,768]{2,1,0:T(8,128)(2,1)S(1)}, u32[]{:S(2)}, u32[]{:S(2)}) async-start(bf16[32,32,768]{2,1,0:T(8,128)(2,1)} %bitcast.13), calls=%async_computation.4 | async-start | bytes 3145728 | tf_op jit(solution)/shard_map/all_to_all | solution.py:459
  364.8 18.6 %all-to-all-done.4 = bf16[32,32,768]{2,1,0:T(8,128)(2,1)S(1)} async-done(((bf16[32,32,768]{2,1,0:T(8,128)(2,1)}), bf16[32,32,768]{2,1,0:T(8,128)(2,1)S(1)}, u32[]{:S(2)}, u32[]{:S(2)}) %all-to-all-start.4) | async-done | bytes 1572896 | tf_op jit(solution)/shard_map/all_to_all | solution.py:459
  384.5 3.8 shard_map.183
  388.4 68.7 %all-reduce = (f32[768]{0:T(1024)}, f32[768]{0:T(1024)}) all-reduce(f32[768]{0:T(1024)S(1)} %reduce, f32[768]{0:T(1024)S(1)} %reduce.1), channel_id=1, replica_groups=mesh['zh'=2,'x'=4,'zl'=2,'y'=4,'c'=2] {'zh','x','zl','y','c'}, use_global_device_ids=true, to_apply=%region_0.1 | all-reduce | flops 1536 | bytes 12288 | tf_op jit(solution)/shard_map/psum | solution.py:499
  460.7 82.3 %all-reduce.4.cloned.1.call-done = (f32[768,2304]{1,0:T(8,128)}, f32[768,768]{1,0:T(8,128)}, f32[768,32]{1,0:T(8,128)}) async-done(((f32[768,2304]{1,0:T(8,128)}, f32[768,768]{1,0:T(8,128)}, f32[768,32]{1,0:T(8,128)}), (f32[768,2304]{1,0:T(8,128)}, f32[768,768]{1,0:T(8,128)}, f32[768,32]{1,0:T(8,128)})) %all-reduce.4.cloned.1.call-update) | async-done | bytes 9535504 | tf_op jit(solution)/shard_map/psum | solution.py:499
  (75 shorter events, 38.4 us)
Async XLA Ops:
  7.2 178.1 %all-gather.7.cloned.1.call-start = ((), (), s32[]{:S(2)}) async-start(), calls=%async_computation.13 | async-start | bytes 5898240 | tf_op jit(solution)/shard_map/all_gather | solution.py:428
  8.6 17.6 %collective-permute-start.1 = (bf16[384,768]{1,0:T(8,128)(2,1)S(1)}, bf16[384,768]{1,0:T(8,128)(2,1)S(1)}, u32[]{:S(2)}, u32[]{:S(2)}) collective-permute-start(bf16[384,768]{1,0:T(8,128)(2,1)S(1)} %get-tuple-element.66), channel_id=1, source_target_pairs={{0,64},{64,0},{1,65},{65,1},{2,66},{66,2},{3,67},{67,3},{4,68},{68... | collective-permute-start | bytes 1769480 | tf_op jit(solution)/shard_map/ppermute | solution.py:427
  26.1 1.7 copy-start.6
  27.2 158.1 %all-gather.5.cloned.1.call-start = ((), (), s32[]{:S(2)}) async-start(), calls=%async_computation.12 | async-start | bytes 5898240 | tf_op jit(solution)/shard_map/all_gather | solution.py:428
  27.9 15.2 %collective-permute-start = (bf16[768,384]{1,0:T(8,128)(2,1)S(1)}, bf16[768,384]{1,0:T(8,128)(2,1)S(1)}, u32[]{:S(2)}, u32[]{:S(2)}) collective-permute-start(bf16[768,384]{1,0:T(8,128)(2,1)S(1)} %get-tuple-element.68), channel_id=1, source_target_pairs={{0,64},{64,0},{1,65},{65,1},{2,66},{66,2},{3,67},{67,3},{4,68},{68... | collective-permute-start | bytes 1769480 | tf_op jit(solution)/shard_map/ppermute | solution.py:427
  92.0 16.4 %copy-start.12 = (s32[1,256,2]{1,2,0:T(2,128)S(1)}, s32[1,256,2]{1,2,0:T(2,128)}, u32[]{:S(2)}) copy-start(s32[1,256,2]{1,2,0:T(2,128)} %param.20) | copy-start | bytes 6148
  103.4 14.0 %all-to-all-start.1 = ((bf16[8,256,128]{2,1,0:T(8,128)(2,1)}), bf16[8,256,128]{2,1,0:T(8,128)(2,1)S(1)}, u32[]{:S(2)}, u32[]{:S(2)}) async-start(bf16[8,256,128]{2,1,0:T(8,128)(2,1)} %get-tuple-element.28), calls=%async_computation.1 | async-start | bytes 1048576 | tf_op jit(solution)/shard_map/all_to_all | solution.py:448
  117.5 13.8 %copy-start.7 = (bf16[768,32]{0,1:T(8,128)(2,1)S(1)}, bf16[768,32]{0,1:T(8,128)(2,1)}, u32[]{:S(2)}) copy-start(bf16[768,32]{0,1:T(8,128)(2,1)} %param.17) | copy-start | bytes 147460
  117.5 14.6 %copy-start.9 = (f32[768]{0:T(1024)S(1)}, f32[768]{0:T(1024)}, u32[]{:S(2)}) copy-start(f32[768]{0:T(1024)} %param.16) | copy-start | bytes 9220
  118.3 35.1 %all-to-all-start.3 = ((bf16[32,32,768]{2,1,0:T(8,128)(2,1)}), bf16[32,32,768]{2,1,0:T(8,128)(2,1)S(1)}, u32[]{:S(2)}, u32[]{:S(2)}) async-start(bf16[32,32,768]{2,1,0:T(8,128)(2,1)} %bitcast.46), calls=%async_computation.3 | async-start | bytes 3145728 | tf_op jit(solution)/shard_map/all_to_all | solution.py:434
  131.2 228.7 %reduce-scatter.5.cloned.1.call-start = ((), (), s32[]{:S(2)}) async-start(), calls=%async_computation.11 | async-start | bytes 5898240 | tf_op jit(solution)/shard_map/reduce_scatter | solution.py:464
  153.4 31.9 %copy-start.1 = (bf16[32,32,768]{2,1,0:T(8,128)(2,1)}, bf16[32,32,768]{2,1,0:T(8,128)(2,1)S(1)}, u32[]{:S(2)}) copy-start(bf16[32,32,768]{2,1,0:T(8,128)(2,1)S(1)} %all-to-all-done.3) | copy-start | bytes 4718596
  234.5 222.7 %reduce-scatter.3.cloned.1.call-start = ((), (), s32[]{:S(2)}) async-start(), calls=%async_computation.10 | async-start | bytes 5898240 | tf_op jit(solution)/shard_map/reduce_scatter | solution.py:464
  235.1 308.0 %all-reduce.4.cloned.1.call-start = ((), (), s32[]{:S(2)}) async-start(), calls=%async_computation.14 | async-start | bytes 19660800 | tf_op jit(solution)/shard_map/psum | solution.py:499
  353.5 11.2 %copy-start.13 = (s32[32]{0:T(128)S(1)}, s32[32]{0:T(128)}, u32[]{:S(2)}) copy-start(s32[32]{0:T(128)} %param.21) | copy-start | bytes 388
  353.5 29.9 %all-to-all-start.4 = ((bf16[32,32,768]{2,1,0:T(8,128)(2,1)}), bf16[32,32,768]{2,1,0:T(8,128)(2,1)S(1)}, u32[]{:S(2)}, u32[]{:S(2)}) async-start(bf16[32,32,768]{2,1,0:T(8,128)(2,1)} %bitcast.13), calls=%async_computation.4 | async-start | bytes 3145728 | tf_op jit(solution)/shard_map/all_to_all | solution.py:459
  361.8 26.5 %copy-start.10 = (f32[1,768]{1,0:T(1,128)S(1)}, f32[1,768]{1,0:T(1,128)}, u32[]{:S(2)}) copy-start(f32[1,768]{1,0:T(1,128)} %get-tuple-element.43) | copy-start | bytes 9220
  361.8 26.6 %copy-start.11 = (f32[1,768]{1,0:T(1,128)S(1)}, f32[1,768]{1,0:T(1,128)}, u32[]{:S(2)}) copy-start(f32[1,768]{1,0:T(1,128)} %get-tuple-element.40) | copy-start | bytes 9220
  361.8 183.2 %collective-permute-start.3 = (bf16[384,768]{1,0:T(8,128)(2,1)}, bf16[384,768]{1,0:T(8,128)(2,1)}, u32[]{:S(2)}, u32[]{:S(2)}) collective-permute-start(bf16[384,768]{1,0:T(8,128)(2,1)} %slice_bitcast_fusion), channel_id=1, source_target_pairs={{0,64},{64,0},{1,65},{65,1},{2,66},{66,2},{3,67},{67,3},{4,68},{68... | collective-permute-start | bytes 1769480 | tf_op jit(solution)/shard_map/ppermute | solution.py:466
  459.1 89.0 %collective-permute-start.2 = (bf16[768,384]{1,0:T(8,128)(2,1)}, bf16[768,384]{1,0:T(8,128)(2,1)}, u32[]{:S(2)}, u32[]{:S(2)}) collective-permute-start(bf16[768,384]{1,0:T(8,128)(2,1)} %split.23), channel_id=1, source_target_pairs={{0,64},{64,0},{1,65},{65,1},{2,66},{66,2},{3,67},{67,3},{4,68},{68... | collective-permute-start | bytes 1769480 | tf_op jit(solution)/shard_map/ppermute | solution.py:466
  543.1 8.3 %slice-start = ((s8[7077888]{0:T(1024)(128)(4,1)}), s8[2883584]{0:T(1024)(128)(4,1)S(1)}, s32[]{:S(2)}) async-start(s8[7077888]{0:T(1024)(128)(4,1)} %bitcast.42), calls=%async_computation.15 | async-start | bytes 5767168
  545.0 3.1 copy-start.5
  546.5 4.9 slice-start.1
  551.4 3.4 copy-start.2
  (4 other events, 4.6 us)
Sparse Core Ops, SparseCore 0:
  27.4 71.7 all-gather.6
  101.4 55.7 all-gather.4
  234.6 49.5 reduce-scatter.4
  286.4 70.4 reduce-scatter.2
  363.3 179.6 all-reduce.3

commit v2 on v1

--- a/solution.py
+++ b/solution.py
@@ -27,7 +27,7 @@
 NEG = -1e30
 
 SEQ = ("zh", "x")
-GROUP = ("zh", "zl", "y", "c")
+MESH = pl.DeviceIdType.MESH
 ALL = ("zh", "x", "zl", "y", "c")
 
 
@@ -198,11 +198,7 @@
     s1 = jnp.sum(earlier * m1, axis=1, keepdims=True)
     s2 = jnp.sum(earlier * m2, axis=1, keepdims=True)
 
-    def column(e, s):
-        place = (e % 2) * (EXPERTS // 2) + e // 2
-        return (place * CAP).astype(F32) + s
-
-    return m1, m2, column(e1, s1), column(e2, s2)
+    return m1, m2, (e1 * CAP).astype(F32) + s1, (e2 * CAP).astype(F32) + s2
 
 
 def chosen(col):
@@ -267,98 +263,395 @@
     return jnp.where(h >= 0, 1.0 - tail, tail), e * (1.0 / math.sqrt(2.0 * math.pi))
 
 
+def div(a, b):
+    return lax.div(a, jnp.int32(b))
+
+
+def rem(a, b):
+    return lax.rem(a, jnp.int32(b))
+
+
+def coords():
+    return tuple(lax.axis_index(a) for a in ALL)
+
+
+def near(x, pair):
+    return x + rem(div(x, 2) + pair, 2) * (3 - 2 * x)
+
+
+def neighbour(x):
+    return x + 1 - 2 * rem(x, 2)
+
+
+def expert_of(zh, x, zl, y):
+    return 4 * (4 * zl + y) + 2 * div(x, 2) + zh
+
+
+def remote(src, dst, send, recv, device):
+    return pltpu.make_async_remote_copy(
+        src_ref=src,
+        dst_ref=dst,
+        send_sem=send,
+        recv_sem=recv,
+        device_id=device,
+        device_id_type=MESH,
+    )
+
+
+def await_bytes(ref, sem):
+    pltpu.make_async_copy(ref, ref, sem).wait()
+
+
+def chip_partner(me, k):
+    zh, x, zl, y, c = me
+    return (
+        rem(zh + div(k, 8), 2),
+        rem(x + rem(div(k, 2), 4), 4),
+        zl,
+        y,
+        rem(c + rem(k, 2), 2),
+    )
+
+
+def row_partner(me, k):
+    zh, x, zl, y, c = me
+    return (
+        rem(zh + rem(div(k, 8), 2), 2),
+        x + div(k, 16) * (3 - 2 * x),
+        rem(zl + rem(div(k, 4), 2), 2),
+        rem(y + rem(k, 4), 4),
+        c,
+    )
+
+
+def head_partner(me, k):
+    zh, x, zl, y, c = me
+    t = rem(zh * 4 + x + k, 8)
+    return t, (div(t, 4), rem(t, 4), zl, y, c)
+
+
+def greet(me, partner, count):
+    barrier = pltpu.get_barrier_semaphore()
+
+    def one(k, carry):
+        pl.semaphore_signal(
+            barrier, inc=1, device_id=partner(me, k), device_id_type=MESH
+        )
+        return carry
+
+    lax.fori_loop(1, count, one, 0)
+    return count - 1
+
+
+def greet_all(*groups):
+    me = coords()
+    total = sum(greet(me, partner, count) for partner, count in groups)
+    pl.semaphore_wait(pltpu.get_barrier_semaphore(), total)
+    return me
+
+
+class HeadSwap:
+    def __init__(self, me, send, recv, sems):
+        self.me, self.send, self.recv, self.sems = me, send, recv, sems
+        self.place = me[0] * 4 + me[1]
+
+    def local(self):
+        s = self.place
+        return pltpu.make_async_copy(
+            self.send.at[s], self.recv.at[s], self.sems.at[0, 0]
+        )
+
+    def copy(self, k):
+        t, device = head_partner(self.me, k)
+        return remote(
+            self.send.at[t],
+            self.recv.at[self.place],
+            self.sems.at[0, k],
+            self.sems.at[1, k],
+            device,
+        )
+
+    def start(self):
+        self.local().start()
+        for k in range(1, 8):
+            self.copy(jnp.int32(k)).start()
+
+    def wait(self):
+        self.local().wait()
+        for k in range(1, 8):
+            self.copy(jnp.int32(k)).wait()
+
+
+class RowSwap:
+    def __init__(self, me, send, recv, sems, back=False):
+        self.me, self.send, self.recv, self.sems = me, send, recv, sems
+        self.back = back
+
+    def ends(self, k):
+        zh, x, zl, y, c = self.me
+        device = row_partner(self.me, k)
+        mirrored = 16 * div(k, 16)
+        if self.back:
+            src = mirrored + 8 * device[0] + 4 * device[2] + device[3]
+            dst = expert_of(zh, x, zl, y)
+        else:
+            src = expert_of(*device[:4])
+            dst = mirrored + 8 * zh + 4 * zl + y
+        rows = lambda n: pl.ds(pl.multiple_of(n * CAP, CAP), CAP)
+        return self.send.at[rows(src)], self.recv.at[rows(dst)], device
+
+    def start(self):
+        src, dst, _ = self.ends(jnp.int32(0))
+        pltpu.make_async_copy(src, dst, self.sems.at[1]).start()
+
+        def one(k, carry):
+            src, dst, device = self.ends(k)
+            remote(src, dst, self.sems.at[0], self.sems.at[1], device).start()
+            return carry
+
+        lax.fori_loop(1, 32, one, 0)
+
+    def wait_recv(self):
+        await_bytes(self.recv, self.sems.at[1])
+
+    def wait_send(self):
+        await_bytes(self.send.at[pl.ds(0, 31 * CAP)], self.sems.at[0])
+
+    def wait(self):
+        self.wait_recv()
+        self.wait_send()
+
+
+def remote_params(n, mb=60):
+    return pltpu.CompilerParams(
+        vmem_limit_bytes=mb * 2**20, collective_id=n, has_side_effects=True
+    )
+
+
+VMEM = pl.BlockSpec(memory_space=pltpu.VMEM)
+ANY = pl.BlockSpec(memory_space=pl.ANY)
+DMA = pltpu.SemaphoreType.DMA
+
+
+class Weights:
+    def __init__(self, me, w_in, w_out, full_in, full_out, sems):
+        self.me, self.refs, self.full, self.sems = me, (w_in, w_out), (full_in, full_out), sems
+
+    def place(self, i, x, zh):
+        at = pl.ds(pl.multiple_of(zh * 384, 128), 384)
+        return self.full[0].at[x, :, at] if i == 0 else self.full[1].at[x, at, :]
+
+    def first(self, i, b):
+        zh, x, zl, y, c = self.me
+        device = (jnp.int32(b), near(x, c), zl, y, zh)
+        copy = remote(
+            self.refs[i].at[b], self.place(i, x, zh), self.sems.at[0, i, b], self.sems.at[1, i, x], device
+        )
+        local = pltpu.make_async_copy(
+            self.refs[i].at[b], self.place(i, x, zh), self.sems.at[1, i, x]
+        )
+        own = jnp.logical_and(
+            jnp.logical_and(zh == b, div(x, 2) == c), zh == c
+        )
+        return copy, local, own
+
+    def start(self, i):
+        for b in range(2):
+            copy, local, own = self.first(i, b)
+            pl.when(own)(local.start)
+            pl.when(jnp.logical_not(own))(copy.start)
+
+    def forward(self, i, x, step):
+        zh, me_x, zl, y, c = self.me
+        piece = self.place(i, x, c)
+        device = (zh, neighbour(me_x), zl, y, c) if step == 2 else (zh, me_x, zl, y, 1 - c)
+        return remote(piece, piece, self.sems.at[2 * step - 2, i, x], self.sems.at[2 * step - 1, i, x], device)
+
+    def sources(self, step):
+        x = self.me[1]
+        if step == 1:
+            return x, 3 - x
+        return neighbour(x), 3 - neighbour(x)
+
+    def second(self, i):
+        for x in self.sources(1):
+            await_bytes(self.place(i, x, self.me[4]), self.sems.at[1, i, x])
+            self.forward(i, x, 2).start()
+            self.forward(i, x, 3).start()
+
+    def third(self, i):
+        for x in self.sources(2):
+            self.forward(i, x, 2).wait_recv()
+            self.forward(i, x, 3).start()
+
+    def finish(self, i):
+        for b in range(2):
+            copy, _, own = self.first(i, b)
+            pl.when(jnp.logical_not(own))(copy.wait_send)
+        for x in self.sources(1):
+            self.forward(i, x, 2).wait_send()
+        for x in range(4):
+            self.forward(i, jnp.int32(x), 3).wait()
+
+
+def front_body(tok_ref, cot_ref, gain1_ref, w_qkv_ref, w_o_ref, gain2_ref, gate_ref, routes_ref, w_in_ref, w_out_ref,
+               qkv_ref, x_ref, c_ref, full_in_ref, full_out_ref, mid_ref, att_ref, gates_ref, ot_ref, lse_ref,
+               qkv_send, o_send, o_recv, x_send, c_send, vt_ref, head_sems, row_sems, weight_sems):
+    me = greet_all((chip_partner, 16), (row_partner, 32))
+    weights = Weights(me, w_in_ref, w_out_ref, full_in_ref, full_out_ref, weight_sems)
+    heads = HeadSwap(me, qkv_send, qkv_ref, head_sems.at[0])
+    heads_back = HeadSwap(me, o_send, o_recv, head_sems.at[1])
+    rows_c = RowSwap(me, c_send, c_ref, row_sems.at[0])
+    rows_x = RowSwap(me, x_send, x_ref, row_sems.at[1])
+    weights.start(0)
+    project_body(tok_ref, gain1_ref, w_qkv_ref, qkv_send)
+    heads.start()
+    deal_body(cot_ref, routes_ref, c_send)
+    weights.start(1)
+    heads.wait()
+    rows_c.start()
+    weights.second(0)
+    attend_forward(rem(me[1], 2), qkv_ref, o_send, ot_ref, lse_ref, vt_ref)
+    heads_back.start()
+    weights.second(1)
+    weights.third(0)
+    heads_back.wait()
+    middle_body(o_recv, tok_ref, w_o_ref, gain2_ref, gate_ref, routes_ref, mid_ref, att_ref, x_send, gates_ref)
+    rows_x.start()
+    weights.third(1)
+    rows_c.wait()
+    weights.finish(0)
+    weights.finish(1)
+    rows_x.wait()
+
+
+def front(tok, cot, gain1, w_qkv, w_o, gain2, gate, routes, w_in, w_out):
+    outs = [
+        ((BLOCKS, ROWS, 384), BF16, VMEM),
+        ((SLOTS, D + EXTRA), BF16, VMEM),
+        ((SLOTS, D), BF16, VMEM),
+        ((4, D, D), BF16, ANY),
+        ((4, D, D), BF16, ANY),
+        ((ROWS, D), F32, VMEM),
+        ((ROWS, D), BF16, VMEM),
+        ((ROWS, 128), F32, VMEM),
+        ((12, 64, ROWS), F32, VMEM),
+        ((12, 8, ROWS), F32, VMEM),
+    ]
+    return pl.pallas_call(
+        front_body,
+        out_shape=[jax.ShapeDtypeStruct(s, t) for s, t, _ in outs],
+        in_specs=[VMEM] * 8 + [ANY] * 2,
+        out_specs=[m for _, _, m in outs],
+        scratch_shapes=[
+            pltpu.VMEM((BLOCKS, ROWS, 384), BF16),
+            pltpu.VMEM((BLOCKS, ROWS, 128), BF16),
+            pltpu.VMEM((BLOCKS, ROWS, 128), BF16),
+            pltpu.VMEM((SLOTS, D + EXTRA), BF16),
+            pltpu.VMEM((SLOTS, D), BF16),
+            pltpu.VMEM((128, BLOCKS * ROWS), BF16),
+            DMA((2, 2, 8)),
+            DMA((2, 2)),
+            DMA((6, 2, 4)),
+        ],
+        compiler_params=remote_params(0),
+    )(tok, cot, gain1, w_qkv, w_o, gain2, gate, routes, w_in, w_out)
+
+
 STEP = 256
-
-
-def expert_body(x_ref, c_ref, win_ref, wout_ref, ret_ref, y_ref, dwin_ref, dwout_ref, g_ref, dh_ref, dx_ref, ya_ref, dg_ref, xg_ref, cg_ref):
-    i = pl.program_id(0)
-    n = pl.num_programs(0)
-
-    @pl.when(i == 0)
-    def _():
-        dx_ref[...] = jnp.zeros_like(dx_ref)
-        ya_ref[...] = jnp.zeros_like(ya_ref)
-        dg_ref[...] = jnp.zeros_like(dg_ref)
-
-    w_in, w_out = win_ref[0], wout_ref[0]
-
-    def rows(r, carry):
-        at = pl.ds(pl.multiple_of(r * STEP, STEP), STEP)
+CHUNKS = 4
+TILES = SLOTS // STEP
+
+
+def row_block(r):
+    return pl.ds(pl.multiple_of(r * STEP, STEP), STEP)
+
+
+def expert_body(x_ref, c_ref, win_ref, wout_ref, ret_ref, y_ref, dwin_ref, dwout_ref,
+                g_ref, dh_ref, dx_ref, dg_ref, xg_ref, cg_ref, ret_send, y_send, sems):
+    me = greet_all((row_partner, 32))
+    rows_ret = RowSwap(me, ret_send, ret_ref, sems.at[0], back=True)
+    rows_y = RowSwap(me, y_send, y_ref, sems.at[1], back=True)
+    dx_ref[...] = jnp.zeros_like(dx_ref)
+    dg_ref[...] = jnp.zeros_like(dg_ref)
+
+    def hidden(n, carry):
+        j, r = div(n, TILES), rem(n, TILES)
+        at = row_block(r)
+        h = dot(x_ref[at, 0:D], win_ref[j])
+        cw = dot(c_ref[at, :], wout_ref[j], 1, 1)
+        phi, density = erf_parts(h)
+        g = h * phi
+        dh = ((phi + h * density) * cw).astype(BF16)
+        g_ref[j, at, :] = g.astype(BF16)
+        dh_ref[j, at, :] = dh
+        prod = g * cw
+        part = prod[:, 0:128]
+        for t in range(1, D // 128):
+            part = part + prod[:, 128 * t : 128 * t + 128]
+        dg_ref[at, :] += part
+        dx_ref[at, :] += dot(dh, win_ref[j], 1, 1)
+        return carry
+
+    lax.fori_loop(0, CHUNKS * TILES, hidden, 0)
+
+    def scale(r, carry):
+        at = row_block(r)
         gate = from_parts(x_ref[at, D:])
-        x, c = x_ref[at, 0:D], c_ref[at, :]
-
-        @pl.when(i == 0)
-        def _():
-            xg_ref[at, :] = x
-            cg_ref[at, :] = (gate * c.astype(F32)).astype(BF16)
-
-        h = dot(x, w_in)
-        cw = dot(cg_ref[at, :], w_out, 1, 1)
-        phi, density = erf_parts(h)
-        g = (h * phi).astype(BF16)
-        dh = ((phi + h * density) * cw).astype(BF16)
-        g_ref[at, :] = g
-        dh_ref[at, :] = dh
-        back = dot(dh, w_in, 1, 1)
-        out = dot(g, w_out)
-        dx_ref[at, :] += back
-        ya_ref[at, :] += out
+        ret_send[at, 0:D] = (dx_ref[at, :] * gate).astype(BF16)
+        ret_send[at, D:] = two_parts(jnp.sum(dg_ref[at, :], axis=1, keepdims=True))
         return carry
 
-    lax.fori_loop(0, SLOTS // STEP, rows, 0)
-    dwin_ref[0] = dot(xg_ref[...], dh_ref[...], 0, 0).astype(BF16)
-    dwout_ref[0] = dot(g_ref[...], cg_ref[...], 0, 0).astype(BF16)
-
-    @pl.when(i == n - 1)
-    def _():
-        def finish(r, carry):
-            at = pl.ds(pl.multiple_of(r * STEP, STEP), STEP)
-            y = ya_ref[at, :].astype(BF16)
-            y_ref[at, :] = y
-            dgate = jnp.sum(
-                c_ref[at, :].astype(F32) * y.astype(F32), axis=1, keepdims=True
-            )
-            ret_ref[at, 0:D] = dx_ref[at, :].astype(BF16)
-            ret_ref[at, D:] = two_parts(dgate)
-            return carry
-
-        lax.fori_loop(0, SLOTS // STEP, finish, 0)
+    lax.fori_loop(0, TILES, scale, 0)
+    rows_ret.start()
+
+    def produce(r, carry):
+        at = row_block(r)
+        gate = from_parts(x_ref[at, D:])
+        xg_ref[at, :] = (x_ref[at, 0:D].astype(F32) * gate).astype(BF16)
+        cg_ref[at, :] = (c_ref[at, :].astype(F32) * gate).astype(BF16)
+        y = dot(g_ref[0, at, :], wout_ref[0])
+        for j in range(1, CHUNKS):
+            y = y + dot(g_ref[j, at, :], wout_ref[j])
+        y_send[at, :] = y.astype(BF16)
+        return carry
+
+    lax.fori_loop(0, TILES, produce, 0)
+    rows_y.start()
+
+    def grads(j, carry):
+        dwin_ref[j] = dot(xg_ref[...], dh_ref[j], 0, 0).astype(BF16)
+        dwout_ref[j] = dot(g_ref[j], cg_ref[...], 0, 0).astype(BF16)
+        return carry
+
+    lax.fori_loop(0, CHUNKS, grads, 0)
+    rows_ret.wait()
+    rows_y.wait()
 
 
 def experts(x, c, w_in, w_out):
-    n, _, width = w_in.shape
-    whole = lambda shape: pl.BlockSpec(shape, lambda i: (0,) * len(shape))
     return pl.pallas_call(
         expert_body,
-        grid=(n,),
         out_shape=[
             jax.ShapeDtypeStruct((SLOTS, D + EXTRA), BF16),
             jax.ShapeDtypeStruct((SLOTS, D), BF16),
-            jax.ShapeDtypeStruct((n, D, width), BF16),
-            jax.ShapeDtypeStruct((n, width, D), BF16),
+            jax.ShapeDtypeStruct((CHUNKS, D, D), BF16),
+            jax.ShapeDtypeStruct((CHUNKS, D, D), BF16),
         ],
-        in_specs=[
-            whole((SLOTS, D + EXTRA)),
-            whole((SLOTS, D)),
-            pl.BlockSpec((1, D, width), lambda i: (i, 0, 0)),
-            pl.BlockSpec((1, width, D), lambda i: (i, 0, 0)),
-        ],
-        out_specs=[
-            whole((SLOTS, D + EXTRA)),
-            whole((SLOTS, D)),
-            pl.BlockSpec((1, D, width), lambda i: (i, 0, 0)),
-            pl.BlockSpec((1, width, D), lambda i: (i, 0, 0)),
-        ],
+        in_specs=[VMEM] * 4,
+        out_specs=[VMEM] * 4,
         scratch_shapes=[
-            pltpu.VMEM((SLOTS, width), BF16),
-            pltpu.VMEM((SLOTS, width), BF16),
-            pltpu.VMEM((SLOTS, D), F32),
+            pltpu.VMEM((CHUNKS, SLOTS, D), BF16),
+            pltpu.VMEM((CHUNKS, SLOTS, D), BF16),
             pltpu.VMEM((SLOTS, D), F32),
             pltpu.VMEM((SLOTS, 128), F32),
             pltpu.VMEM((SLOTS, D), BF16),
             pltpu.VMEM((SLOTS, D), BF16),
+            pltpu.VMEM((SLOTS, D + EXTRA), BF16),
+            pltpu.VMEM((SLOTS, D), BF16),
+            DMA((2, 2)),
         ],
-        compiler_params=params(60),
+        compiler_params=remote_params(1),
     )(x, c, w_in, w_out)
 
 
@@ -375,7 +668,7 @@
     a2 = (unit * gain_ref[...]).astype(BF16)
     high = dlogits.astype(BF16)
     low = (dlogits - high.astype(F32)).astype(BF16)
-    gate_grad_ref[...] = dot(a2, high, 0, 0) + dot(a2, low, 0, 0)
+    gate_grad_ref[...] = dot(high, a2, 0, 0) + dot(low, a2, 0, 0)
     gate_w = gate_w_ref[...]
     da2 = dot(s1 + s2, ret_ref[:, 0:D]) + dot(high, gate_w, 1, 1) + dot(low, gate_w, 1, 1)
     gain_grad_ref[...] = jnp.sum(da2 * unit, axis=0, keepdims=True)
@@ -411,132 +704,332 @@
     tok_grad_ref[...] = dmid_ref[...] + norm_back(da1, gain_ref[...], unit, inv)
 
 
-def on_device(tokens, cotangent, gain_first, w_qkv, w_o, gain_second, w_gate, w_in, w_out, routes, frozen):
-    zh = lax.axis_index("zh")
-    s = zh * 4 + lax.axis_index("x")
-    e = (lax.axis_index("zl") * 4 + lax.axis_index("y")) * 2 + lax.axis_index("c")
-    half = s % 2
-    tok, cot, routes = tokens[0], cotangent[0], routes[0]
-    gain1, gain2 = gain_first.reshape(1, D), gain_second.reshape(1, D)
-
-    swap = [(0, 1), (1, 0)]
-
-    def gather(w, axis):
-        own = lax.dynamic_index_in_dim(w, zh, 0, keepdims=False)
-        other = lax.dynamic_index_in_dim(w, 1 - zh, 0, keepdims=False)
-        got = lax.ppermute(other, "zh", swap)
-        return lax.all_gather(jnp.concatenate([own, got], axis=axis), "x")
-
-    w_in_full = gather(w_in, 1)
-    w_out_full = gather(w_out, 0)
-
-    c_send = call(deal_body, [((SLOTS, D), BF16)], 2)(cot, routes)[0]
-    c_rows = lax.all_to_all(c_send.reshape(32, CAP, D), GROUP, 0, 0, tiled=True)
-
-    qkv_send = call(project_body, [((BLOCKS, ROWS, 384), BF16)], 3)(tok, gain1, w_qkv)[0]
-    qkv = lax.all_to_all(qkv_send, SEQ, 0, 0, tiled=True)
-
-    def fwd(*refs):
-        attend_forward(lax.axis_index("x") % 2, *refs)
-
-    o_send, ot, lse = call(
-        fwd,
-        [((BLOCKS, ROWS, 128), BF16), ((12, 64, ROWS), F32), ((12, 8, ROWS), F32)],
-        1,
-        [pltpu.VMEM((128, BLOCKS * ROWS), BF16)],
-    )(qkv)
-    o = lax.all_to_all(o_send, SEQ, 0, 0, tiled=True)
-    mid, att, x_send, gates = call(
-        middle_body,
-        [((ROWS, D), F32), ((ROWS, D), BF16), ((SLOTS, D + EXTRA), BF16), ((ROWS, 128), F32)],
-        6,
-    )(o, tok, w_o, gain2, w_gate, routes)
-    x_rows = lax.all_to_all(x_send.reshape(32, CAP, D + EXTRA), GROUP, 0, 0, tiled=True)
-    ret, y, dw_in, dw_out = experts(
-        x_rows.reshape(SLOTS, D + EXTRA), c_rows.reshape(SLOTS, D), w_in_full, w_out_full
-    )
-    ret = lax.all_to_all(ret.reshape(32, CAP, D + EXTRA), GROUP, 0, 0, tiled=True).reshape(SLOTS, D + EXTRA)
-    y = lax.all_to_all(y.reshape(32, CAP, D), GROUP, 0, 0, tiled=True).reshape(SLOTS, D)
-
-    keep = (1 - lax.dynamic_slice_in_dim(frozen, 2 * e, 2)).astype(F32)
-
-    def scatter(dw, axis):
-        mine = lax.psum_scatter(dw, "x", scatter_dimension=0, tiled=False)
-        own, other = jnp.split(mine, 2, axis=axis)
-        got = lax.ppermute(other, "zh", swap)
-        first = jnp.where(zh == 0, own, got).astype(F32)
-        second = jnp.where(zh == 0, got, own).astype(F32)
-        return jnp.stack([first, second]) * keep[:, None, None]
-
-    w_in_grad = scatter(dw_in, 1)
-    w_out_grad = scatter(dw_out, 0)
-
-    do_send, dmid, o_grad, gate_grad, gain2_grad = call(
-        back_body,
-        [((BLOCKS, ROWS, 128), BF16), ((ROWS, D), F32), ((D, D), F32), ((D, EXPERTS), F32), ((1, D), F32)],
-        9,
-    )(ret, cot, routes, gates, mid, att, gain2, w_gate, w_o)
-    do = lax.all_to_all(do_send, SEQ, 0, 0, tiled=True)
-
-    def bwd(*refs):
-        attend_backward(lax.axis_index("x") % 2, *refs)
-
-    dqkv_send = call(
-        bwd,
-        [((BLOCKS, ROWS, 384), BF16)],
-        4,
-        [
+def rear_body(ret_ref, cot_ref, routes_ref, gates_ref, mid_ref, att_ref, gain2_ref, gate_w_ref, w_o_ref,
+              qkv_ref, ot_ref, lse_ref, tok_ref, gain1_ref, w_qkv_ref,
+              tok_grad_ref, grads_ref, small_ref,
+              dmid_ref, do_send, do_recv, dqkv_send, dqkv_recv, kt_ref, dk_ref, dv_ref, sems):
+    me = greet_all((lambda m, k: head_partner(m, k)[1], 8))
+    heads = HeadSwap(me, do_send, do_recv, sems.at[0])
+    heads_back = HeadSwap(me, dqkv_send, dqkv_recv, sems.at[1])
+    small_ref[...] = jnp.zeros_like(small_ref)
+    back_body(ret_ref, cot_ref, routes_ref, gates_ref, mid_ref, att_ref, gain2_ref, gate_w_ref, w_o_ref,
+              do_send, dmid_ref, grads_ref.at[:, 3 * D : 4 * D], small_ref.at[0:32], small_ref.at[32:33])
+    heads.start()
+    heads.wait()
+    attend_backward(rem(me[1], 2), qkv_ref, do_recv, ot_ref, lse_ref, dqkv_send, kt_ref, dk_ref, dv_ref)
+    heads_back.start()
+    heads_back.wait()
+    finish_body(dqkv_recv, tok_ref, gain1_ref, w_qkv_ref, dmid_ref, tok_grad_ref,
+                grads_ref.at[:, 0 : 3 * D], small_ref.at[40:41])
+
+
+def rear(*args):
+    return pl.pallas_call(
+        rear_body,
+        out_shape=[
+            jax.ShapeDtypeStruct((ROWS, D), F32),
+            jax.ShapeDtypeStruct((D, 4 * D), F32),
+            jax.ShapeDtypeStruct((48, D), F32),
+        ],
+        in_specs=[VMEM] * len(args),
+        out_specs=[VMEM] * 3,
+        scratch_shapes=[
+            pltpu.VMEM((ROWS, D), F32),
+            pltpu.VMEM((BLOCKS, ROWS, 128), BF16),
+            pltpu.VMEM((BLOCKS, ROWS, 128), BF16),
+            pltpu.VMEM((BLOCKS, ROWS, 384), BF16),
+            pltpu.VMEM((BLOCKS, ROWS, 384), BF16),
             pltpu.VMEM((128, BLOCKS * ROWS), BF16),
             pltpu.VMEM((BLOCKS * ROWS, 128), F32),
             pltpu.VMEM((BLOCKS * ROWS, 128), F32),
+            DMA((2, 2, 8)),
         ],
-    )(qkv, do, ot, lse)[0]
-    dqkv = lax.all_to_all(dqkv_send, SEQ, 0, 0, tiled=True)
+        compiler_params=remote_params(2),
+    )(*args)
+
+
+def collect_body(dwin_ref, dwout_ref, fin_in, fin_out, got1_in, got1_out, sum_in, sum_out, send_in, send_out, got2_in, got2_out, sems):
+    me = greet_all((chip_partner, 16))
+    zh, x, zl, y, c = me
+    dw, got1, total = (dwin_ref, dwout_ref), (got1_in, got1_out), (sum_in, sum_out)
+    send, got2, fin = (send_in, send_out), (got2_in, got2_out), (fin_in, fin_out)
+
+    def half(i, n, xs):
+        at = pl.ds(pl.multiple_of(n * 384, 128), 384)
+        return dw[i].at[xs, :, at] if i == 0 else dw[i].at[xs, at, :]
+
+    def first(i, xs):
+        return remote(half(i, 1 - c, xs), got1[i].at[xs], sems.at[0, i, xs], sems.at[1, i, xs], (zh, x, zl, y, 1 - c))
+
+    def second(i, j):
+        return remote(send[i].at[j], got2[i].at[j], sems.at[2, i, j], sems.at[3, i, j], (zh, neighbour(x), zl, y, c))
+
+    xs3 = (x, 3 - x)
+
+    def third(i, j):
+        pair = div(x, 2)
+        copy = remote(total[i].at[j], fin[i].at[zh], sems.at[4, i, j], sems.at[5, i, zh], (c, xs3[j], zl, y, pair))
+        local = pltpu.make_async_copy(total[i].at[j], fin[i].at[zh], sems.at[5, i, zh])
+        own = jnp.logical_and(jnp.logical_and(zh == c, pair == c), j == 0)
+        return copy, local, own
+
+    for i in range(2):
+        for xs in (neighbour(x), 3 - neighbour(x), x, 3 - x):
+            first(i, xs).start()
+    for i in range(2):
+        for j, xs in enumerate((neighbour(x), 3 - neighbour(x))):
+            first(i, xs).wait_recv()
+            send[i][j] = (half(i, c, xs)[...].astype(F32) + got1[i][xs].astype(F32)).astype(BF16)
+            second(i, j).start()
+    for i in range(2):
+        for j, xs in enumerate(xs3):
+            first(i, xs).wait_recv()
+            second(i, j).wait_recv()
+            total[i][j] = (half(i, c, xs)[...].astype(F32) + got1[i][xs].astype(F32) + got2[i][j].astype(F32)).astype(BF16)
+            copy, local, own = third(i, j)
+            pl.when(own)(local.start)
+            pl.when(jnp.logical_not(own))(copy.start)
+    for i in range(2):
+        for xs in range(4):
+            first(i, jnp.int32(xs)).wait_send()
+        for j in range(2):
+            second(i, j).wait_send()
+            copy, _, own = third(i, j)
+            pl.when(jnp.logical_not(own))(copy.wait_send)
+        for b in range(2):
+            await_bytes(fin[i].at[b], sems.at[5, i, b])
+
+
+def collect(dw_in, dw_out):
+    shapes = [(D, 384), (384, D)]
+    buf = lambda n: [pltpu.VMEM((n,) + s, BF16) for s in shapes]
+    return pl.pallas_call(
+        collect_body,
+        out_shape=[jax.ShapeDtypeStruct((2,) + s, BF16) for s in shapes],
+        in_specs=[VMEM] * 2,
+        out_specs=[VMEM] * 2,
+        scratch_shapes=buf(4) + buf(2) + buf(2) + buf(2) + [DMA((6, 2, 4))],
+        compiler_params=remote_params(3),
+    )(dw_in, dw_out)
+
+
+AXES = (1, 3, 2)
+
+
+def axis_place(me, a):
+    zh, x, zl, y, c = me
+    return (x, y, 2 * zh + zl)[a]
+
+
+def axis_peer(me, a, k):
+    zh, x, zl, y, c = me
+    p = rem(axis_place(me, a) + k, 4)
+    if a == 0:
+        return p, (zh, p, zl, y, c)
+    if a == 1:
+        return p, (zh, x, zl, p, c)
+    return p, (div(p, 2), x, rem(p, 2), y, c)
+
+
+def total_body(grads_ref, small_ref, out_ref, small_out,
+               s0, r0, a0, s1, r1, a1, s2, r2, a2, r3, sa, sr, sems, small_sems):
+    me = coords()
+    zh, x, zl, y, c = me
+    sibling = (zh, x, zl, y, 1 - c)
+    barrier = pltpu.get_barrier_semaphore()
+    pl.semaphore_signal(barrier, inc=1, device_id=sibling, device_id_type=MESH)
+    for a in range(3):
+        for k in range(1, 4):
+            pl.semaphore_signal(barrier, inc=1, device_id=axis_peer(me, a, jnp.int32(k))[1], device_id_type=MESH)
+    pl.semaphore_wait(barrier, 10)
+
+    def lanes(n, w, base=0):
+        return pl.ds(pl.multiple_of(base + n * w, 128), w)
+
+    def rows(n, w, base=0):
+        return pl.ds(pl.multiple_of(base + n * w, 16), w)
+
+    place = [[axis_place(me, (g + t) % 3) for t in range(3)] for g in range(3)]
+
+    def swap0(g):
+        return remote(s0.at[g], r0.at[g], sems.at[0, g, 0], sems.at[1, g, 0], sibling)
+
+    def small0():
+        return remote(small_ref, sr.at[0], small_sems.at[0, 0], small_sems.at[1, 0], sibling)
+
+    for g in range(3):
+        s0[g] = grads_ref[:, lanes(1 - c, 512, 1024 * g)].astype(BF16)
+        swap0(g).start()
+    small0().start()
+
+    def scatter(stage, g, k, src, dst):
+        p, device = axis_peer(me, (g + stage - 1) % 3, k)
+        n = 2 * stage
+        return remote(src(p), dst.at[g, k - 1], sems.at[n, g, k], sems.at[n + 1, g, k], device)
+
+    ks = range(1, 4)
+
+    def scatter1(g, k):
+        return scatter(1, g, k, lambda p: s1.at[g, rows(p, 192)], r1)
+
+    def scatter2(g, k):
+        return scatter(2, g, k, lambda p: s2.at[g, :, lanes(p, 128)], r2)
+
+    def scatter3(g, k):
+        return scatter(3, g, k, lambda p: a2.at[g, rows(p, 48)], r3)
+
+    def small_step(a, k):
+        n = 3 * a + k
+        return remote(sa.at[a], sr.at[1 + 4 * a + axis_place(me, a)], small_sems.at[0, n], small_sems.at[1, n],
+                      axis_peer(me, a, jnp.int32(k))[1])
+
+    def small_sum(a):
+        for k in ks:
+            small_step(a, k).wait_recv()
+        sr[1 + 4 * a + axis_place(me, a)] = sa[a]
+        return (sr[1 + 4 * a] + sr[2 + 4 * a]) + (sr[3 + 4 * a] + sr[4 + 4 * a])
+
+    for g in range(3):
+        swap0(g).wait_recv()
+        a0[g] = grads_ref[:, lanes(c, 512, 1024 * g)] + r0[g].astype(F32)
+        s1[g] = a0[g].astype(BF16)
+        for k in ks:
+            scatter1(g, jnp.int32(k)).start()
+    small0().wait_recv()
+    sa[0] = small_ref[...] + sr[0]
+    for k in ks:
+        small_step(0, k).start()
+    for g in range(3):
+        for k in ks:
+            scatter1(g, jnp.int32(k)).wait_recv()
+        mine = a0[g, rows(place[g][0], 192), :]
+        for k in ks:
+            mine = mine + r1[g, k - 1].astype(F32)
+        a1[g] = mine
+        s2[g] = mine.astype(BF16)
+        for k in ks:
+            scatter2(g, jnp.int32(k)).start()
+    sa[1] = small_sum(0)
+    for k in ks:
+        small_step(1, k).start()
+    for g in range(3):
+        for k in ks:
+            scatter2(g, jnp.int32(k)).wait_recv()
+        mine = a1[g, :, lanes(place[g][1], 128)]
+        for k in ks:
+            mine = mine + r2[g, k - 1].astype(F32)
+        a2[g] = mine
+        for k in ks:
+            scatter3(g, jnp.int32(k)).start()
+    sa[2] = small_sum(1)
+    for k in ks:
+        small_step(2, k).start()
+
+    def block(g, stage):
+        i, j, k = place[g]
+        if stage == 3:
+            return out_ref.at[rows(4 * i + k, 48), lanes(j, 128, 1024 * g + 512 * c)]
+        if stage == 2:
+            return out_ref.at[rows(i, 192), lanes(j, 128, 1024 * g + 512 * c)]
+        if stage == 1:
+            return out_ref.at[rows(i, 192), lanes(c, 512, 1024 * g)]
+        return out_ref.at[:, lanes(c, 512, 1024 * g)]
+
+    def gather(g, stage, k):
+        n = 8 + 2 * stage
+        if stage == 0:
+            device = sibling
+        else:
+            device = axis_peer(me, (g + stage - 1) % 3, k)[1]
+        return remote(block(g, stage), block(g, stage), sems.at[n, g, k], sems.at[n + 1, g, k], device)
+
+    for g in range(3):
+        for k in ks:
+            scatter3(g, jnp.int32(k)).wait_recv()
+        mine = a2[g, rows(place[g][2], 48), :]
+        for k in ks:
+            mine = mine + r3[g, k - 1]
+        block(g, 3)[...] = mine.astype(BF16)
+        for k in ks:
+            gather(g, 3, jnp.int32(k)).start()
+    for stage in (2, 1, 0):
+        for g in range(3):
+            for k in ks:
+                gather(g, stage + 1, jnp.int32(k)).wait()
+            for k in ks if stage else (0,):
+                gather(g, stage, jnp.int32(k)).start()
+    small_out[...] = small_sum(2)
+    small0().wait_send()
+    for k in ks:
+        for a in range(3):
+            small_step(a, k).wait_send()
+    for g in range(3):
+        swap0(g).wait_send()
+        for k in ks:
+            scatter1(g, jnp.int32(k)).wait_send()
+            scatter2(g, jnp.int32(k)).wait_send()
+            scatter3(g, jnp.int32(k)).wait_send()
+        gather(g, 0, jnp.int32(0)).wait()
+
+
+def totals(grads, small):
+    return pl.pallas_call(
+        total_body,
+        out_shape=[jax.ShapeDtypeStruct((D, 4 * D), BF16), jax.ShapeDtypeStruct((48, D), F32)],
+        in_specs=[VMEM] * 2,
+        out_specs=[VMEM] * 2,
+        scratch_shapes=[
+            pltpu.VMEM((3, D, 512), BF16),
+            pltpu.VMEM((3, D, 512), BF16),
+            pltpu.VMEM((3, D, 512), F32),
+            pltpu.VMEM((3, D, 512), BF16),
+            pltpu.VMEM((3, 3, 192, 512), BF16),
+            pltpu.VMEM((3, 192, 512), F32),
+            pltpu.VMEM((3, 192, 512), BF16),
+            pltpu.VMEM((3, 3, 192, 128), BF16),
+            pltpu.VMEM((3, 192, 128), F32),
+            pltpu.VMEM((3, 3, 48, 128), F32),
+            pltpu.VMEM((3, 48, D), F32),
+            pltpu.VMEM((13, 48, D), F32),
+            DMA((16, 3, 4)),
+            DMA((2, 10)),
+        ],
+        compiler_params=remote_params(4),
+    )(grads, small)
+
+
+def on_device(tokens, cotangent, gain_first, w_qkv, w_o, gain_second, w_gate, w_in, w_out, routes, frozen):
+    e = (lax.axis_index("zl") * 4 + lax.axis_index("y")) * 2 + lax.axis_index("c")
+    tok, cot, routes = tokens[0], cotangent[0], routes[0]
+    gain1, gain2 = gain_first.reshape(1, D), gain_second.reshape(1, D)
+    qkv, x_rows, c_rows, w_in_full, w_out_full, mid, att, gates, ot, lse = front(
+        tok, cot, gain1, w_qkv, w_o, gain2, w_gate, routes, w_in, w_out
+    )
+    ret, y, dw_in, dw_out = experts(x_rows, c_rows, w_in_full, w_out_full)
+    keep = (1 - lax.dynamic_slice_in_dim(frozen, 2 * e, 2)).astype(F32)
+    tok_grad, grads, small = rear(
+        ret, cot, routes, gates, mid, att, gain2, w_gate, w_o, qkv, ot, lse, tok, gain1, w_qkv
+    )
+    w_in_grad, w_out_grad = collect(dw_in, dw_out)
     out = call(out_body, [((ROWS, D), BF16)], 4)(y, mid, gates, routes)[0]
-    tok_grad, qkv_grad, gain1_grad = call(
-        finish_body, [((ROWS, D), F32), ((D, 3 * D), F32), ((1, D), F32)], 5
-    )(dqkv, tok, gain1, w_qkv, dmid)
-    qkv_grad, o_grad, gate_grad, gain1_grad, gain2_grad = lax.psum(
-        (qkv_grad, o_grad, gate_grad, gain1_grad, gain2_grad), ALL
-    )
+    grads, small = totals(grads, small)
     return (
         out[None],
         tok_grad[None],
-        gain1_grad.reshape(D),
-        qkv_grad,
-        o_grad,
-        gain2_grad.reshape(D),
-        gate_grad * (1 - frozen).astype(F32)[None, :],
-        w_in_grad,
-        w_out_grad,
+        small[40],
+        grads[:, : 3 * D].astype(F32),
+        grads[:, 3 * D :].astype(F32),
+        small[32],
+        small[:32].T * (1 - frozen).astype(F32)[None, :],
+        w_in_grad.astype(F32) * keep[:, None, None],
+        w_out_grad.astype(F32) * keep[:, None, None],
     )
 
 
 def solution(mesh):
     fine = Mesh(mesh.devices.reshape(2, 4, 2, 4, 2), ALL)
     seq, exp = ("zh", "x"), ("zl", "y", "c")
-    in_specs = (
-        P(exp, seq, None),
-        P(exp, seq, None),
-        P(),
-        P(),
-        P(),
-        P(),
-        P(),
-        P(exp, None, seq),
-        P(exp, seq, None),
-        P(exp, seq, None),
-        P(),
-    )
-    out_specs = (
-        P(exp, seq, None),
-        P(exp, seq, None),
-        P(),
-        P(),
-        P(),
-        P(),
-        P(),
-        P(exp, None, seq),
-        P(exp, seq, None),
-    )
+    rows, rest = P(exp, seq, None), P()
+    in_specs = (rows, rows, rest, rest, rest, rest, rest, P(exp, None, seq), rows, rows, rest)
+    out_specs = (rows, rows, rest, rest, rest, rest, rest, P(exp, None, seq), rows)
     return jax.shard_map(on_device, mesh=fine, in_specs=in_specs, out_specs=out_specs, check_vma=False)

time: 572 us -> 447 us (0.78)
  Pallas kernels: 106 us -> 417 us
  blocking collectives: 232 us -> 0 us
  waiting for transfers between devices: 148 us -> 0 us
  starting transfers between devices: 36.2 us -> 0 us
  between operations: 14.4 us -> 1.16 us
  local copies, waits for them, and re-layouts: 17.1 us -> 7.13 us
    pallas_call x8 -> x5, Pallas kernels: 102 us -> 413 us  [the longest x1 118 us: front(): pl.pallas_call(front_body, out_shape=[jax.ShapeDtypeStruct(s, t) for s, t...]
    all_to_all x5 -> x0, blocking collectives: 163 us -> none  [the longest x1 42.5 us: on_device(): qkv = lax.all_to_all(qkv_send, SEQ, 0, 0, tiled=True)]
    psum x1 -> x0, waiting for transfers between devices: 82.3 us -> none  [on_device(): lax.psum((qkv_grad, o_grad, gate_grad, gain1_grad, gain2_grad), ALL)]
    psum x1 -> x0, blocking collectives: 68.7 us -> none  [on_device(): lax.psum((qkv_grad, o_grad, gate_grad, gain1_grad, gain2_grad), ALL)]
    all_to_all x3 -> x0, waiting for transfers between devices: 39.2 us -> none  [the longest x1 18.6 us: on_device(): lax.all_to_all(y.reshape(32, CAP, D), GROUP, 0, 0, tiled=True)]
    ppermute x4 -> x0, waiting for transfers between devices: 25.5 us -> none  [the longest x2 25.5 us: gather(): got = lax.ppermute(other, 'zh', swap)]
    all_to_all x3 -> x0, starting transfers between devices: 24.3 us -> none  [the longest x1 12.9 us: on_device(): c_rows = lax.all_to_all(c_send.reshape(32, CAP, D), GROUP, 0, 0, tiled=True)]
    ppermute x4 -> x0, starting transfers between devices: 11.8 us -> none  [the longest x2 7.23 us: gather(): got = lax.ppermute(other, 'zh', swap)]
  transfers between devices with their start and end apart: 12 -> 0, of which waited for: 6 -> 0; matrix products, arithmetic and copies ran while one was open for 2% -> 0% of each run, Pallas kernels for 10% -> 0%
where the time goes in v2:
time: 447 us; the launch traced here: 439 us
  Pallas kernels  417 us (93%)
  other arithmetic  13.8 us (3%)
  local copies, waits for them, and re-layouts  7.13 us (2%)
    pallas_call x1, Pallas kernels, front(): pl.pallas_call(front_body, out_shape=[jax.ShapeDtypeStruct(s, t) for s, t...  118 us
    pallas_call x1, Pallas kernels, collect(): pl.pallas_call(collect_body, out_shape=[jax.ShapeDtypeStruct((2,) + s, BF...  87.6 us
    pallas_call x1, Pallas kernels, experts(): pl.pallas_call(expert_body, out_shape=[jax.ShapeDtypeStruct((SLOTS, D + E...  79.5 us
    pallas_call x1, Pallas kernels, totals(): pl.pallas_call(total_body, out_shape=[jax.ShapeDtypeStruct((D, 4 * D), BF...  73.5 us
    pallas_call x1, Pallas kernels, rear(): pl.pallas_call(rear_body, out_shape=[jax.ShapeDtypeStruct((ROWS, D), F32)...  54.3 us

profile of v2, /device:TPU:1, one launch (start us, length us, event | category | flops | bytes accessed | tf_op | source)
XLA Modules:
  0.0 439.0 jit_solution(13468303657229713426)
XLA Ops:
  0.6 1.5 copy.20
  2.1 1.6 copy.21.gate_ref.gate_w_ref
  3.7 1.3 reshape.26.gain1_ref
  5.0 1.3 reshape.27.gain2_ref
  6.3 118.1 %shard_map.178 = (bf16[8,256,384]{2,1,0:T(8,128)(2,1)}, bf16[1024,896]{1,0:T(8,128)(2,1)}, bf16[1024,768]{1,0:T(8,128)(2,1)}, bf16[4,768,768]{2,1,0:T(8,128)(2,1...) custom-call(bf16[256,768]{1,0:T(8,128)(2,1)} %bitcast.10, ...), custom_call_target="tpu_custom_call" | custom-call | tf_op jit(solution)/shard_map/pallas_call | solution.py:541
  124.4 79.5 %shard_map.179 = (bf16[1024,896]{1,0:T(8,128)(2,1)}, bf16[1024,768]{1,0:T(8,128)(2,1)}, bf16[4,768,768]{2,1,0:T(8,128)(2,1)}, bf16[4,768,768]{2,1,0:T(8,128)(2,1)}) custom-call(bf16[1024,896]{1,0:T(8,128)(2,1)} %get-tuple-element.30.x_ref, bf16[1024,768]{1,0:T(8,128)(2,1)} %get-tuple-element.31.c_ref, bf16[4,768,768]{2,1,0:T(8,128)(2,1)} %get-tuple-element.32.win_ref, ...), custom_call_target="tpu_custom_call" | custom-call | tf_op jit(solution)/shard_map/pallas_call | solution.py:633
  203.9 0.0 copy-start.3
  204.0 87.6 %shard_map.183 = (bf16[2,768,384]{2,1,0:T(8,128)(2,1)}, bf16[2,384,768]{2,1,0:T(8,128)(2,1)}) custom-call(bf16[4,768,768]{2,1,0:T(8,128)(2,1)} %get-tuple-element.47.dwin_ref, bf16[4,768,768]{2,1,0:T(8,128)(2,1)} %get-tuple-element.48.dwout_ref), custom_call_target="tpu_custom_call" | custom-call | tf_op jit(solution)/shard_map/pallas_call | solution.py:806
  291.6 0.0 copy-start
  291.6 0.0 copy-done.3
  291.6 0.1 subtract_convert_fusion
  291.7 3.0 convert_multiply_fusion
  294.7 0.0 copy-done
  294.7 1.6 convert_multiply_fusion.1
  296.3 54.3 %shard_map.181 = (f32[256,768]{1,0:T(8,128)}, f32[768,3072]{1,0:T(8,128)}, f32[48,768]{1,0:T(8,128)}) custom-call(bf16[1024,896]{1,0:T(8,128)(2,1)} %get-tuple-element.37.ret_ref, bf16[256,768]{1,0:T(8,128)(2,1)} %bitcast.13, s32[256,2]{1,0:T(8,128)} %bitcast.8, f32[256,128]{1,0:T(8,128)} %get-tuple-element.36.gates_ref, ...), custom_call_target="tpu_custom_call" | custom-call | tf_op jit(solution)/shard_map/pallas_call | solution.py:727
  350.6 73.5 %shard_map.182 = (bf16[768,3072]{1,0:T(8,128)(2,1)}, f32[48,768]{1,0:T(8,128)}) custom-call(f32[768,3072]{1,0:T(8,128)} %get-tuple-element.43.grads_ref, f32[48,768]{1,0:T(8,128)} %get-tuple-element.44.small_ref), custom_call_target="tpu_custom_call" | custom-call | tf_op jit(solution)/shard_map/pallas_call | solution.py:976
  424.1 5.5 %slice_convert_fusion = f32[768,2304]{1,0:T(8,128)} fusion(bf16[768,3072]{1,0:T(8,128)(2,1)} %get-tuple-element.46), kind=kLoop, calls=%fused_computation | loop fusion | flops 1769472 | bytes 10616832 | tf_op jit(solution)/shard_map/convert_element_type | solution.py:1020
  429.6 2.9 slice_convert_fusion.1
  432.5 0.0 copy-done.2
  432.5 0.7 multiply_bitcast_fusion
  433.2 0.6 slice_reduce_fusion
  433.8 3.9 shard_map.180
  437.7 0.0 copy-done.1
  437.7 0.9 copy.24
  (3 shorter events, 0.0 us)
Async XLA Ops:
  203.9 87.6 %copy-start.3 = (s32[32]{0:T(128)S(1)}, s32[32]{0:T(128)}, u32[]{:S(2)}) copy-start(s32[32]{0:T(128)} %param.21) | copy-start | bytes 388
  291.6 3.1 copy-start
  429.6 2.9 copy-start.2
  432.5 5.2 %copy-start.1 = (f32[256,768]{1,0:T(8,128)S(1)}, f32[256,768]{1,0:T(8,128)}, u32[]{:S(2)}) copy-start(f32[256,768]{1,0:T(8,128)} %get-tuple-element.42) | copy-start | bytes 2359300
